TPU v7x, 128 devices: a whole 4x4x4 slice. The times are simulated.
128 devices in a mesh: dp: 8 (over x, z_lo), seq: 16 (over y, z_hi, core).
Axes of the slice: x: 4, y: 4, z: 4 (z_hi: 2, z_lo: 2; z = z_hi * 2 + z_lo), core: 2. Of those that a mesh axis runs over, the one named last changes fastest.
Arguments:
- tokens: bfloat16 [16384, 2048], P(('dp', 'seq')), may hold values from -6 to 6
- cotangent: bfloat16 [16384, 2048], P(('dp', 'seq')), may hold values from -6 to 6
- lengths: int32 [8, 5], P('dp'), may hold values from 129 to 1024, as said below
- qkv_weight: bfloat16 [2048, 6144], P('dp'), may hold values from -0.125 to 0.125
- out_weight: bfloat16 [2048, 2048], P('dp'), may hold values from -0.5 to 0.5
- up_weight: bfloat16 [2048, 8192], P('dp'), may hold values from -0.125 to 0.125
- down_weight: bfloat16 [2048, 8192], P('dp'), may hold values from -0.0625 to 0.0625
- bias_query: bfloat16 [2048], replicated, may hold values from -3 to 3
- bias_value: bfloat16 [2048], replicated, may hold values from -2 to 2
- out_bias: bfloat16 [2048], replicated, may hold values from -1 to 1
- up_bias: bfloat16 [8192], replicated, may hold values from -3 to 3
- down_bias: bfloat16 [2048], replicated, may hold values from -1 to 1
- norm_gain_one: bfloat16 [2048], replicated, may hold values from 0.5 to 1.5
- norm_shift_one: bfloat16 [2048], replicated, may hold values from -1 to 1
- norm_gain_two: bfloat16 [2048], replicated, may hold values from 0.5 to 1.5
- norm_shift_two: bfloat16 [2048], replicated, may hold values from -1 to 1
Outputs:
- output: bfloat16 [16384, 2048], P(('dp', 'seq'))
- input_grad: bfloat16 [16384, 2048], P(('dp', 'seq'))
- qkv_grad: float32 [2048, 6144], P('dp')
- out_grad: float32 [2048, 2048], P('dp')
- up_grad: float32 [2048, 8192], P('dp')
- down_grad: float32 [2048, 8192], P('dp')
- bias_query_grad: float32 [2048], replicated
- bias_value_grad: float32 [2048], replicated
- out_bias_grad: float32 [2048], replicated
- up_bias_grad: float32 [8192], replicated
- down_bias_grad: float32 [2048], replicated
- norm_gain_one_grad: float32 [2048], replicated
- norm_shift_one_grad: float32 [2048], replicated
- norm_gain_two_grad: float32 [2048], replicated
- norm_shift_two_grad: float32 [2048], replicated
Inputs may be any that keep to these rules, and one draw needn't show every extreme that they name: Column 0 is a group's prompt length, at least 961 and exactly 1024 in some group; the other columns are continuation lengths, at least 129, with exactly 256 in one continuation of every group.
All inputs are finite; a program needn't handle non-finite values.
Results may differ from a plain program's by a relative error of at most 0.024.
Values may be sent and summed in bfloat16 or wider, within the bound.
A program may use at most 576 MiB of HBM per device.

v0:
```python
import jax
import jax.numpy as jnp
from jax import lax
from jax.sharding import PartitionSpec as P

H = 16
HEAD = 128
CONT = 256


epsilon = 1e-05


def norm_rows(values, gain, shift):
    average = jnp.mean(values, axis=-1, keepdims=True)
    centred = values - average
    variance = jnp.mean(centred * centred, axis=-1, keepdims=True)
    return centred * lax.rsqrt(variance + epsilon) * gain + shift


def gelu_tanh(values):
    return jax.nn.gelu(values, approximate=True)


def row_layout(lengths_row, devices, half, cont):
    per_device = 2 * half
    rows = jnp.arange(per_device * devices, dtype=jnp.int32)
    device_of = rows // per_device
    local = rows % per_device
    is_prompt = local < half
    flat = device_of * half + jnp.where(is_prompt, local, local - half)
    continuation = jnp.where(is_prompt, -1, flat // cont)
    inner = jnp.where(is_prompt, flat, flat % cont)
    prompt_len = lengths_row[0]
    own_len = jnp.where(
        is_prompt, prompt_len, jnp.take(lengths_row, 1 + jnp.maximum(continuation, 0))
    )
    position = jnp.where(is_prompt, inner, prompt_len + inner)
    live = inner < own_len
    return (continuation, inner, position, live)


def allowed_pairs(cont_query, inner_query, cont_key, inner_key, live_key):
    prompt_key = cont_key[None, :] < 0
    earlier = inner_key[None, :] <= inner_query[:, None]
    from_prompt = prompt_key & ((cont_query[:, None] >= 0) | earlier)
    same_cont = ~prompt_key & (cont_key[None, :] == cont_query[:, None]) & earlier
    return live_key[None, :] & (from_prompt | same_cont)


def contract_rows(left, right):
    return lax.dot_general(
        left, right, (((0,), (0,)), ((), ())), preferred_element_type=jnp.float32
    )


def times_transpose(left, right):
    return lax.dot_general(
        left, right, (((1,), (1,)), ((), ())), preferred_element_type=jnp.float32
    )


def body(
    tokens,
    cotangent,
    lengths,
    qkv_weight,
    out_weight,
    up_weight,
    down_weight,
    bias_query,
    bias_value,
    out_bias,
    up_bias,
    down_bias,
    norm_gain_one,
    norm_shift_one,
    norm_gain_two,
    norm_shift_two,
):
    seq_count = lax.axis_size("seq")
    per_device, width = tokens.shape
    local_heads = H // seq_count
    group_rows = per_device * seq_count
    scale = HEAD ** (-0.5)
    query_b = bias_query.astype(jnp.float32)
    value_b = bias_value.astype(jnp.float32)
    out_b = out_bias.astype(jnp.float32)
    up_b = up_bias.astype(jnp.float32)
    down_b = down_bias.astype(jnp.float32)
    gain_one = norm_gain_one.astype(jnp.float32)
    shift_one = norm_shift_one.astype(jnp.float32)
    gain_two = norm_gain_two.astype(jnp.float32)
    shift_two = norm_shift_two.astype(jnp.float32)
    token_vals = tokens.astype(jnp.float32)
    qkv_full, out_full = (
        lax.all_gather(qkv_weight, "dp", axis=0, tiled=True),
        lax.all_gather(out_weight, "dp", axis=0, tiled=True),
    )
    normed, norm_one_back = jax.vjp(norm_rows, token_vals, gain_one, shift_one)
    normed_low = normed.astype(jnp.bfloat16)
    bias_cat = jnp.concatenate([query_b, jnp.zeros_like(query_b), value_b])
    mixed = (jnp.dot(normed_low, qkv_full, preferred_element_type=jnp.float32) + bias_cat).astype(
        jnp.bfloat16
    )
    spread = lax.all_to_all(
        mixed.reshape(per_device, 3, H, HEAD), "seq", split_axis=2, concat_axis=0, tiled=True
    )
    queries = spread[:, 0]
    keys_all = spread[:, 1]
    values_all = spread[:, 2]
    continuation, inner, position, live = row_layout(lengths[0], seq_count, per_device // 2, CONT)
    head_ids = lax.axis_index("seq") * local_heads + jnp.arange(local_heads, dtype=jnp.int32)
    slopes = jnp.exp2(-8.0 * (head_ids + 1).astype(jnp.float32) / H)
    block = min(512, group_rows)
    count = group_rows // block
    starts = jnp.arange(count, dtype=jnp.int32) * block

    def scores_for(query_block, start):
        cont_query = lax.dynamic_slice_in_dim(continuation, start, block)
        inner_query = lax.dynamic_slice_in_dim(inner, start, block)
        pos_query = lax.dynamic_slice_in_dim(position, start, block)
        raw = (
            jnp.einsum("qhd,khd->hqk", query_block, keys_all, preferred_element_type=jnp.float32)
            * scale
        )
        distance = (pos_query[:, None] - position[None, :]).astype(jnp.float32)
        raw = raw - slopes[:, None, None] * distance[None]
        mask = allowed_pairs(cont_query, inner_query, continuation, inner, live)
        return jnp.where(mask[None], raw, -1e30)

    def forward_block(start):
        query_block = lax.dynamic_slice_in_dim(queries, start, block, 0)
        scores = scores_for(query_block, start)
        top = jnp.max(scores, axis=-1, keepdims=True)
        total = jnp.sum(jnp.exp(scores - top), axis=-1, keepdims=True)
        log_total = top + jnp.log(total)
        probs = jnp.exp(scores - log_total)
        out_block = jnp.einsum(
            "hqk,khd->qhd",
            probs.astype(jnp.bfloat16),
            values_all,
            preferred_element_type=jnp.float32,
        )
        return (out_block.astype(jnp.bfloat16), log_total[..., 0])

    out_blocks, log_totals = lax.map(forward_block, starts)
    heads_out = out_blocks.reshape(group_rows, local_heads, HEAD)
    attended_low = lax.all_to_all(
        heads_out, "seq", split_axis=0, concat_axis=1, tiled=True
    ).reshape(per_device, width)
    attended = jnp.dot(attended_low, out_full, preferred_element_type=jnp.float32) + out_b
    middle = token_vals + attended
    up_full, down_full = (
        lax.all_gather(up_weight, "dp", axis=0, tiled=True),
        lax.all_gather(down_weight, "dp", axis=0, tiled=True),
    )
    normed_two, norm_two_back = jax.vjp(norm_rows, middle, gain_two, shift_two)
    normed_two_low = normed_two.astype(jnp.bfloat16)
    hidden_pre = jnp.dot(normed_two_low, up_full, preferred_element_type=jnp.float32) + up_b
    activated, gelu_back = jax.vjp(gelu_tanh, hidden_pre)
    activated_low = activated.astype(jnp.bfloat16)
    branch = times_transpose(activated_low, down_full) + down_b
    output = (middle + branch).astype(jnp.bfloat16)
    cot_vals = cotangent.astype(jnp.float32)
    branch_grad = cot_vals.astype(jnp.bfloat16)
    down_bias_grad = jnp.sum(branch_grad.astype(jnp.float32), axis=0)
    act_grad = jnp.dot(branch_grad, down_full, preferred_element_type=jnp.float32)
    (pre_grad,) = gelu_back(act_grad)
    pre_low = pre_grad.astype(jnp.bfloat16)
    up_bias_grad = jnp.sum(pre_low.astype(jnp.float32), axis=0)
    norm_two_grad = times_transpose(pre_low, up_full)
    mid_norm, gain_two_grad, shift_two_grad = norm_two_back(norm_two_grad)
    middle_grad = cot_vals + mid_norm
    mlp_part = lax.psum_scatter(
        jnp.concatenate(
            [contract_rows(normed_two_low, pre_low), contract_rows(branch_grad, activated_low)],
            axis=1,
        ).astype(jnp.bfloat16),
        "dp",
        scatter_dimension=0,
        tiled=True,
    )
    attn_grad_low = middle_grad.astype(jnp.bfloat16)
    out_bias_grad = jnp.sum(attn_grad_low.astype(jnp.float32), axis=0)
    qkv_again, out_again = (
        lax.all_gather(qkv_weight, "dp", axis=0, tiled=True),
        lax.all_gather(out_weight, "dp", axis=0, tiled=True),
    )
    heads_grad_tok = times_transpose(attn_grad_low, out_again).astype(jnp.bfloat16)
    head_grads = lax.all_to_all(
        heads_grad_tok.reshape(per_device, H, HEAD), "seq", split_axis=1, concat_axis=0, tiled=True
    )

    def backward_block(carry, inputs):
        key_grad, value_grad = carry
        start, log_total = inputs
        query_block = lax.dynamic_slice_in_dim(queries, start, block, 0)
        grad_block = lax.dynamic_slice_in_dim(head_grads, start, block, 0)
        scores = scores_for(query_block, start)
        probs = jnp.exp(scores - log_total[..., None])
        probs_low = probs.astype(jnp.bfloat16)
        value_grad = value_grad + jnp.einsum(
            "hqk,qhd->khd", probs_low, grad_block, preferred_element_type=jnp.float32
        )
        prob_grad = jnp.einsum(
            "qhd,khd->hqk", grad_block, values_all, preferred_element_type=jnp.float32
        )
        inner_sum = jnp.sum(probs * prob_grad, axis=-1, keepdims=True)
        score_grad = (probs * (prob_grad - inner_sum)).astype(jnp.bfloat16)
        query_grad = (
            jnp.einsum("hqk,khd->qhd", score_grad, keys_all, preferred_element_type=jnp.float32)
            * scale
        )
        key_grad = (
            key_grad
            + jnp.einsum(
                "hqk,qhd->khd", score_grad, query_block, preferred_element_type=jnp.float32
            )
            * scale
        )
        return ((key_grad, value_grad), query_grad)

    empty = jnp.zeros((group_rows, local_heads, HEAD), jnp.float32)
    (key_grad, value_grad), query_grads = lax.scan(
        backward_block, (empty, empty), (starts, log_totals)
    )
    query_grad = query_grads.reshape(group_rows, local_heads, HEAD)
    mixed_grad_heads = jnp.stack([query_grad, key_grad, value_grad], axis=1).astype(jnp.bfloat16)
    mixed_grad = lax.all_to_all(
        mixed_grad_heads, "seq", split_axis=0, concat_axis=2, tiled=True
    ).reshape(per_device, 3 * width)
    mixed_grad_vals = mixed_grad.astype(jnp.float32)
    bias_query_grad = jnp.sum(mixed_grad_vals[:, :width], axis=0)
    bias_value_grad = jnp.sum(mixed_grad_vals[:, 2 * width :], axis=0)
    normed_grad = times_transpose(mixed_grad, qkv_again)
    token_norm, gain_one_grad, shift_one_grad = norm_one_back(normed_grad)
    input_grad = (middle_grad + token_norm).astype(jnp.bfloat16)
    attn_part = lax.psum_scatter(
        jnp.concatenate(
            [contract_rows(normed_low, mixed_grad), contract_rows(attended_low, attn_grad_low)],
            axis=1,
        ).astype(jnp.bfloat16),
        "dp",
        scatter_dimension=0,
        tiled=True,
    )
    mlp_sum, attn_sum = (
        lax.psum(mlp_part, "seq").astype(jnp.float32),
        lax.psum(attn_part, "seq").astype(jnp.float32),
    )
    small_sums = lax.psum(
        (
            bias_query_grad,
            bias_value_grad,
            out_bias_grad,
            up_bias_grad,
            down_bias_grad,
            gain_one_grad,
            shift_one_grad,
            gain_two_grad,
            shift_two_grad,
        ),
        ("dp", "seq"),
    )
    ff_width = up_full.shape[1]
    return (
        output,
        input_grad,
        attn_sum[:, : 3 * width],
        attn_sum[:, 3 * width :],
        mlp_sum[:, :ff_width],
        mlp_sum[:, ff_width:],
        small_sums[0],
        small_sums[1],
        small_sums[2],
        small_sums[3],
        small_sums[4],
        small_sums[5],
        small_sums[6],
        small_sums[7],
        small_sums[8],
    )


def solution(mesh):
    in_specs = (
        P(("dp", "seq"), None),
        P(("dp", "seq"), None),
        P("dp", None),
        P("dp", None),
        P("dp", None),
        P("dp", None),
        P("dp", None),
        P(),
        P(),
        P(),
        P(),
        P(),
        P(),
        P(),
        P(),
        P(),
    )
    out_specs = (
        P(("dp", "seq"), None),
        P(("dp", "seq"), None),
        P("dp", None),
        P("dp", None),
        P("dp", None),
        P("dp", None),
        P(),
        P(),
        P(),
        P(),
        P(),
        P(),
        P(),
        P(),
        P(),
    )
    return jax.shard_map(body, mesh=mesh, in_specs=in_specs, out_specs=out_specs, check_vma=False)
```

profile of v0, /device:TPU:1, one launch (start us, length us, event | category | flops | bytes accessed | tf_op | source)
XLA Modules:
  0.0 4557.5 jit_solution(1850204853573094486)
XLA Ops:
  10.6 485.3 %all-gather.5.cloned.1.call-done = bf16[2048,6144]{1,0:T(8,128)(2,1)} async-done(((bf16[256,6144]{1,0:T(8,128)(2,1)}), bf16[2048,6144]{1,0:T(8,128)(2,1)}) %all-gather.5.cloned.1.call-update) | async-done | bytes 25165840 | tf_op jit(solution)/shard_map/all_gather | solution.py:97
  496.0 11.8 fusion.53
  509.7 7.3 all-to-all-start
  518.4 3.3 compare_select_fusion.3
  522.4 21.9 all-to-all-done
  544.6 28.4 while.29
  547.4 2.7 fusion.135
  554.5 2.7 fusion.135
  561.6 2.7 fusion.135
  568.7 2.7 fusion.135
  575.6 7.6 all-to-all-start.1
  583.3 14.1 all-to-all-done.1
  598.3 91.2 %all-gather.7.cloned.1.call-done = bf16[2048,2048]{1,0:T(8,128)(2,1)} async-done(((bf16[256,2048]{1,0:T(8,128)(2,1)}), bf16[2048,2048]{1,0:T(8,128)(2,1)}) %all-gather.7.cloned.1.call-update) | async-done | bytes 8388624 | tf_op jit(solution)/shard_map/all_gather | solution.py:98
  689.5 4.8 fusion.94
  694.6 642.3 %all-gather.11.cloned.1.call-done = bf16[2048,8192]{1,0:T(8,128)(2,1)} async-done(((bf16[256,8192]{1,0:T(8,128)(2,1)}), bf16[2048,8192]{1,0:T(8,128)(2,1)}) %all-gather.11.cloned.1.call-update) | async-done | bytes 33554448 | tf_op jit(solution)/shard_map/all_gather | solution.py:156
  1336.9 17.1 fusion.95
  1353.9 625.7 %all-gather.9.cloned.1.call-done = bf16[2048,8192]{1,0:T(8,128)(2,1)} async-done(((bf16[256,8192]{1,0:T(8,128)(2,1)}), bf16[2048,8192]{1,0:T(8,128)(2,1)}) %all-gather.9.cloned.1.call-update) | async-done | bytes 33554448 | tf_op jit(solution)/shard_map/all_gather | solution.py:155
  1979.7 18.7 convert_reduce_fusion
  1998.4 19.7 multiply_reduce_fusion.1
  2019.7 2.3 convert_reduce_fusion.3
  2021.9 6.5 fusion.54
  2029.4 15.9 all-to-all-start.2
  2045.3 11.0 all-to-all-done.2
  2056.4 46.0 %while.30 = (s32[]{:T(128)}, f32[2048,1,128]{0,2,1:T(8,128)S(1)}, f32[2048,1,128]{0,2,1:T(8,128)S(1)}, bf16[4,512,1,128]{3,1,2,0:T(8,128)(2,1)}, s32[4]{0:T(128)...) while((s32[]{:T(128)}, f32[2048,1,128]{0,2,1:T(8,128)S(1)}, ...), condition=%wide.region_12.13_spmd.clone.clone, body=%wide.region_10.12_spmd.clone.clone.sunk | while | flops 1365577728 | bytes 46472572 | solution.py:225
  2059.2 1.6 fusion.145
  2060.9 3.4 multiply_reduce_fusion.5
  2072.4 3.4 multiply_reduce_fusion.5
  2083.9 3.4 multiply_reduce_fusion.5
  2095.4 3.4 multiply_reduce_fusion.5
  2105.1 10.7 copy.80
  2115.8 5.1 all-to-all-start.3
  2120.9 6.8 convolution_convert_fusion.2
  2127.7 21.7 all-to-all-done.3
  2150.7 1.9 copy.82
  2152.7 12.0 convolution_convert_fusion.1
  2164.7 22.6 pad_maximum_fusion.1
  2188.5 15.9 convolution_convert_fusion
  2204.4 16.1 convert_bitcast_fusion
  2220.5 44.2 pad_maximum_fusion
  2264.8 563.1 %reduce-scatter.3.cloned.1.call-done = bf16[256,8192]{1,0:T(8,128)(2,1)} async-done(((bf16[2048,8192]{1,0:T(8,128)(2,1)}), bf16[256,8192]{1,0:T(8,128)(2,1)}) %reduce-scatter.3.cloned.1.call-update) | async-done | bytes 4194320 | tf_op jit(solution)/shard_map/reduce_scatter | solution.py:239
  2827.9 1273.8 %reduce-scatter.5.cloned.1.call-done = bf16[256,16384]{1,0:T(8,128)(2,1)} async-done(((bf16[2048,16384]{1,0:T(8,128)(2,1)}), bf16[256,16384]{1,0:T(8,128)(2,1)}) %reduce-scatter.5.cloned.1.call-update) | async-done | bytes 8388624 | tf_op jit(solution)/shard_map/reduce_scatter | solution.py:175
  4102.4 18.3 fusion.48
  4122.1 13.8 fusion.85
  4137.0 3.4 convert_reduce_fusion.2
  4140.4 248.1 %all-reduce.7.cloned.1.call-done = (bf16[256,8192]{1,0:T(8,128)(2,1)}, bf16[256,16384]{1,0:T(8,128)(2,1)}) async-done(((bf16[256,8192]{1,0:T(8,128)(2,1)}, bf16[256,16384]{1,0:T(8,128)(2,1)}), (bf16[256,8192]{1,0:T(8,128)(2,1)}, bf16[256,16384]{1,0:T(8,128)(2,1)})) %all-reduce.7.cloned.1.call-update) | async-done | bytes 12582928 | tf_op jit(solution)/shard_map/psum | solution.py:250
  4388.6 12.0 fusion.92
  4402.1 3.4 slice.56
  4405.5 133.0 %all-reduce.5.cloned.1.call-done = (f32[2048]{0:T(1024)}, f32[2048]{0:T(1024)}, f32[2048]{0:T(1024)}, f32[8192]{0:T(1024)}, f32[2048]{0:T(1024)}, /*index=5*/f32...) async-done(((f32[2048]{0:T(1024)}, f32[2048]{0:T(1024)}, f32[2048]{0:T(1024)}, f32[8192]{0:T(1024)}, f32[2048]{0:T(1024)}, /*index=5*/f32[2048]{0:T(1024)}, ...) | async-done | bytes 98320 | tf_op jit(solution)/shard_map/psum | solution.py:252
  (256 shorter events, 67.5 us)
Async XLA Ops:
  7.2 488.8 %all-gather.5.cloned.1.call-start = ((), (), s32[]{:S(2)}) async-start(), calls=%async_computation.6 | async-start | bytes 28311552 | tf_op jit(solution)/shard_map/all_gather | solution.py:97
  7.9 681.5 %all-gather.7.cloned.1.call-start = ((), (), s32[]{:S(2)}) async-start(), calls=%async_computation.7 | async-start | bytes 9437184 | tf_op jit(solution)/shard_map/all_gather | solution.py:98
  8.7 1328.1 %all-gather.11.cloned.1.call-start = ((), (), s32[]{:S(2)}) async-start(), calls=%async_computation.9 | async-start | bytes 37748736 | tf_op jit(solution)/shard_map/all_gather | solution.py:156
  9.4 1970.2 %all-gather.9.cloned.1.call-start = ((), (), s32[]{:S(2)}) async-start(), calls=%async_computation.8 | async-start | bytes 37748736 | tf_op jit(solution)/shard_map/all_gather | solution.py:155
  10.1 497.7 %copy-start.14 = (f32[2048]{0:T(1024)}, f32[2048]{0:T(1024)S(1)}, u32[]{:S(2)}) copy-start(f32[2048]{0:T(1024)S(1)} %convert_element_type.123) | copy-start | bytes 24580
  10.1 497.7 %copy-start.18 = (f32[2048]{0:T(1024)}, f32[2048]{0:T(1024)S(1)}, u32[]{:S(2)}) copy-start(f32[2048]{0:T(1024)S(1)} %convert_element_type.124) | copy-start | bytes 24580
  10.3 497.4 %copy-start.20 = (f32[128]{0:T(128)}, f32[128]{0:T(128)S(1)}, u32[]{:S(2)}) copy-start(f32[128]{0:T(128)S(1)} %broadcast_multiply_fusion.1) | copy-start | bytes 1540
  10.6 497.1 %copy-start.36 = (f32[128]{0:T(128)}, f32[128]{0:T(128)S(1)}, u32[]{:S(2)}) copy-start(f32[128]{0:T(128)S(1)} %fusion.60) | copy-start | bytes 1540
  10.6 497.1 %copy-start.22 = (f32[128]{0:T(128)}, f32[128]{0:T(128)S(1)}, u32[]{:S(2)}) copy-start(f32[128]{0:T(128)S(1)} %fusion.80) | copy-start | bytes 1540
  507.8 9.3 copy-start.25
  509.7 34.6 all-to-all-start
  544.6 38.6 copy-start.30
  544.6 38.6 copy-start.31
  544.6 38.6 copy-start.32
  544.6 38.6 copy-start.24
  573.1 10.2 copy-start.12
  573.1 116.4 %copy-start.3 = (bf16[2048,1,128]{2,0,1:T(8,128)(2,1)}, bf16[2048,1,128]{2,0,1:T(8,128)(2,1)S(1)}, u32[]{:S(2)}) copy-start(bf16[2048,1,128]{2,0,1:T(8,128)(2,1)S(1)} %get-tuple-element.756) | copy-start | bytes 1572868
  575.6 21.8 all-to-all-start.1
  598.3 96.0 %copy-start.6 = (bf16[128,16,1,128]{0,3,1,2:T(8,128)(2,1)}, bf16[128,16,1,128]{0,3,1,2:T(8,128)(2,1)S(1)}, u32[]{:S(2)}) copy-start(bf16[128,16,1,128]{0,3,1,2:T(8,128)(2,1)S(1)} %copy.75) | copy-start | bytes 1572868
  689.5 647.4 %copy-start.9 = (bf16[128,2048]{1,0:T(8,128)(2,1)S(1)}, bf16[128,2048]{1,0:T(8,128)(2,1)}, u32[]{:S(2)}) copy-start(bf16[128,2048]{1,0:T(8,128)(2,1)} %param.21) | copy-start | bytes 1572868
  694.3 1323.8 %copy-start.1 = (f32[128,2048]{1,0:T(8,128)}, f32[128,2048]{1,0:T(8,128)S(1)}, u32[]{:S(2)}) copy-start(f32[128,2048]{1,0:T(8,128)S(1)} %get-tuple-element.411) | copy-start | bytes 3145732
  2019.7 8.8 copy-start.8
  2019.7 8.7 copy-start.34
  2021.9 6.5 copy-start.11
  2029.4 27.0 all-to-all-start.2
  2058.9 1.9 copy-start.4
  2058.9 1.9 copy-start.13
  2064.7 1.6 copy-start.16
  2070.4 1.9 copy-start.4
  2070.4 1.9 copy-start.13
  2081.9 1.9 copy-start.4
  2081.9 1.9 copy-start.13
  2093.4 1.9 copy-start.4
  2093.4 1.9 copy-start.13
  2105.0 15.8 copy-start.7
  2115.8 33.6 all-to-all-start.3
  2120.8 707.1 %reduce-scatter.3.cloned.1.call-start = ((), (), s32[]{:S(2)}) async-start(), calls=%async_computation.10 | async-start | bytes 37748736 | tf_op jit(solution)/shard_map/reduce_scatter | solution.py:239
  2127.7 25.0 copy-start.15
  2127.7 25.0 copy-start.19
  2127.7 25.0 copy-start.21
  2127.7 25.0 copy-start.23
  2187.3 1914.4 %reduce-scatter.5.cloned.1.call-start = ((), (), s32[]{:S(2)}) async-start(), calls=%async_computation.11 | async-start | bytes 75497472 | tf_op jit(solution)/shard_map/reduce_scatter | solution.py:175
  2188.5 15.9 copy-start.10
  2264.7 2123.8 %all-reduce.7.cloned.1.call-start = ((), (), s32[]{:S(2)}) async-start(), calls=%async_computation.13 | async-start | bytes 25165824 | tf_op jit(solution)/shard_map/psum | solution.py:250
  4101.7 436.8 %all-reduce.5.cloned.1.call-start = ((), (), s32[]{:S(2)}) async-start(), calls=%async_computation.12 | async-start | bytes 196608 | tf_op jit(solution)/shard_map/psum | solution.py:252
  4122.1 13.8 copy-start.37
  4122.1 14.9 copy-start.35
  4388.6 12.0 copy-start.5
  (14 other events, 16.8 us)
Sparse Core Ops, SparseCore 0:
  9.7 486.2 all-gather.4
  497.6 191.8 all-gather.6
  691.1 645.6 all-gather.10
  1338.3 641.2 all-gather.8
  2187.5 640.4 reduce-scatter.2
  2830.4 1271.2 reduce-scatter.4
  4104.3 284.2 all-reduce.6
  4396.1 142.3 all-reduce.4
where the time goes:
time: 4570 us; the launch traced here: 4560 us
  waiting for transfers between devices  4130 us (90%)
  matrix products  208 us (5%)
  other arithmetic  89.7 us (2%)
  local copies, waits for them, and re-layouts  58.5 us (1%)
    reduce_scatter x1, waiting for transfers between devices, body(): lax.psum_scatter(jnp.concatenate([contract_rows(normed_two_low, pre_low),...  1270 us
    all_gather x1, waiting for transfers between devices, body(): lax.all_gather(down_weight, 'dp', axis=0, tiled=True)  642 us
    all_gather x1, waiting for transfers between devices, body(): lax.all_gather(up_weight, 'dp', axis=0, tiled=True)  626 us
    reduce_scatter x1, waiting for transfers between devices, body(): lax.psum_scatter(jnp.concatenate([contract_rows(normed_low, mixed_grad),...  563 us
    all_gather x1, waiting for transfers between devices, body(): lax.all_gather(qkv_weight, 'dp', axis=0, tiled=True)  485 us
    psum x1, waiting for transfers between devices, body(): lax.psum(attn_part, 'seq').astype(jnp.float32)  248 us
    psum x1, waiting for transfers between devices, body(): lax.psum((bias_query_grad, bias_value_grad, out_bias_grad, up_bias_grad,...  133 us
  transfers between devices with their start and end apart: 12, of which 12 were waited for; matrix products, arithmetic and copies ran while one was open for 4% of the time, Pallas kernels for 0%

commit v1 on v0

v1 whole, which is shorter than its diff:
```python
import functools

import jax
import jax.numpy as jnp
from jax import lax
from jax.experimental import pallas as pl
from jax.experimental.pallas import tpu as pltpu
from jax.sharding import Mesh, PartitionSpec as P

H = 16
HEAD = 128
CONT = 256
AXES = ("x", "zl", "y", "zh", "c")
MESH = pl.DeviceIdType.MESH
ANY = pl.BlockSpec(memory_space=pl.ANY)
BF = jnp.bfloat16
F32 = jnp.float32
STEPS = (1, -1, 2)
epsilon = 1e-05


def place():
    return {a: lax.axis_index(a) for a in AXES}


def moved(p, x=0, y=0, z=0, c=0):
    zz = lax.rem(p["zh"] * 2 + p["zl"] + z + 4, 4)
    return {
        "x": lax.rem(p["x"] + x + 4, 4),
        "zl": lax.rem(zz, 2),
        "y": lax.rem(p["y"] + y + 4, 4),
        "zh": zz // 2,
        "c": lax.rem(p["c"] + c, 2),
    }


def greet(peers):
    bar = pltpu.get_barrier_semaphore()
    for q in peers:
        pl.semaphore_signal(bar, inc=1, device_id=q, device_id_type=MESH)
    pl.semaphore_wait(bar, len(peers))


def put(src, dst, send, recv, to):
    return pltpu.make_async_remote_copy(
        src_ref=src, dst_ref=dst, send_sem=send, recv_sem=recv, device_id=to, device_id_type=MESH
    )


def params(cid, mb=56):
    return pltpu.CompilerParams(
        collective_id=cid, has_side_effects=True, vmem_limit_bytes=mb * 2**20
    )


DMA = pltpu.SemaphoreType.DMA


def team_gather_kernel(a, out, ss, rs, cs, cr, ls):
    p = place()
    c = p["c"]
    rows = a.shape[0]
    h = rows // 2
    up, down, twin = moved(p, y=1), moved(p, y=-1), moved(p, c=1)
    greet((up, down, twin))
    lo, hi = pl.ds(0, h), pl.ds(h, h)

    def block(dy):
        return lax.rem(p["y"] + dy + 4, 4) * 2 + c

    me = block(0)
    own = pltpu.make_async_copy(a, out.at[me], ls)
    own.start()
    s_lo = put(a.at[lo], out.at[me, lo], ss.at[0], rs.at[0], up)
    s_hi = put(a.at[hi], out.at[me, hi], ss.at[1], rs.at[1], down)
    s_lo.start()
    s_hi.start()
    t_own = put(a, out.at[me], cs.at[6], cr.at[6], twin)
    t_own.start()
    s_lo2 = put(a.at[hi], out.at[me, hi], ss.at[2], rs.at[2], up)
    s_hi2 = put(a.at[lo], out.at[me, lo], ss.at[3], rs.at[3], down)
    twins = [t_own]

    def share(k, b, part):
        cp = put(out.at[b, part], out.at[b, part], cs.at[k], cr.at[k], twin)
        cp.start()
        twins.append(cp)

    s_lo.wait_recv()
    f_lo = put(out.at[block(-1), lo], out.at[block(-1), lo], ss.at[4], rs.at[4], up)
    f_lo.start()
    s_lo2.start()
    s_hi.wait_recv()
    f_hi = put(out.at[block(1), hi], out.at[block(1), hi], ss.at[5], rs.at[5], down)
    f_hi.start()
    s_hi2.start()
    share(0, block(-1), lo)
    share(1, block(1), hi)
    f_lo.wait_recv()
    share(2, block(2), lo)
    f_hi.wait_recv()
    share(3, block(2), hi)
    s_lo2.wait_recv()
    share(4, block(-1), hi)
    s_hi2.wait_recv()
    share(5, block(1), lo)
    for cp in twins:
        cp.wait_recv()
    for cp in twins + [s_lo, s_hi, s_lo2, s_hi2, f_lo, f_hi]:
        cp.wait_send()
    own.wait()


def team_gather(a, cid):
    return pl.pallas_call(
        team_gather_kernel,
        out_shape=jax.ShapeDtypeStruct((8,) + a.shape, a.dtype),
        in_specs=[ANY],
        out_specs=ANY,
        scratch_shapes=[DMA((6,)), DMA((6,)), DMA((7,)), DMA((7,)), DMA],
        compiler_params=params(cid),
    )(a)


def add_rows(dst, dst_rows, terms, step=16):
    n = dst_rows[1]

    def body(i, _):
        o = pl.multiple_of(i * step, step)
        total = None
        for ref, base in terms:
            v = ref[pl.ds(base + o, step)].astype(F32)
            total = v if total is None else total + v
        dst[pl.ds(dst_rows[0] + o, step)] = total.astype(dst.dtype)
        return 0

    lax.fori_loop(0, n // step, body, 0)


def team_reduce_kernel(a, out, mine, other, keep, r2, r1, ss, rs, cs, cr, ls):
    p = place()
    c = p["c"]
    rows = a.shape[1]
    h = rows // 2
    up, down, twin = moved(p, y=1), moved(p, y=-1), moved(p, c=1)
    greet((up, down, twin))
    lo, hi = pl.ds(0, h), pl.ds(h, h)
    order = (2, 1, -1, 0)

    def yy(d):
        return lax.rem(p["y"] + d + 4, 4)

    sends, loads = [], []
    for k, d in enumerate(order):
        cp = put(a.at[yy(d) * 2 + 1 - c], other.at[k], cs.at[k], cr.at[k], twin)
        cp.start()
        sends.append(cp)
        ld = pltpu.make_async_copy(a.at[yy(d) * 2 + c], mine.at[k], ls.at[k])
        ld.start()
        loads.append(ld)

    def chip_sum(k):
        sends[k].wait_recv()
        loads[k].wait()
        add_rows(keep.at[k], (0, rows), [(mine.at[k], 0), (other.at[k], 0)])

    chip_sum(0)
    f_lo = put(keep.at[0, lo], r2.at[lo], ss.at[0], rs.at[0], up)
    f_hi = put(keep.at[0, hi], r2.at[hi], ss.at[1], rs.at[1], down)
    f_lo.start()
    f_hi.start()
    chip_sum(1)
    u_hi = put(keep.at[1, hi], r1.at[0, hi], ss.at[2], rs.at[2], up)
    u_hi.start()
    chip_sum(2)
    d_lo = put(keep.at[2, lo], r1.at[1, lo], ss.at[3], rs.at[3], down)
    d_lo.start()
    chip_sum(3)
    f_lo.wait_recv()
    add_rows(keep.at[1], (0, h), [(keep.at[1], 0), (r2, 0)])
    u_lo = put(keep.at[1, lo], r1.at[0, lo], ss.at[4], rs.at[4], up)
    u_lo.start()
    f_hi.wait_recv()
    add_rows(keep.at[2], (h, h), [(keep.at[2], h), (r2, h)])
    d_hi = put(keep.at[2, hi], r1.at[1, hi], ss.at[5], rs.at[5], down)
    d_hi.start()
    for cp in (u_hi, d_lo, u_lo, d_hi):
        cp.wait_recv()
    add_rows(out, (0, rows), [(keep.at[3], 0), (r1.at[0], 0), (r1.at[1], 0)])
    for cp in sends + [f_lo, f_hi, u_hi, d_lo, u_lo, d_hi]:
        cp.wait_send()


def team_reduce(a, cid):
    _, rows, cols = a.shape
    return pl.pallas_call(
        team_reduce_kernel,
        out_shape=jax.ShapeDtypeStruct((rows, cols), F32),
        in_specs=[ANY],
        out_specs=pl.BlockSpec(memory_space=pltpu.VMEM),
        scratch_shapes=[
            pltpu.VMEM((4, rows, cols), BF),
            pltpu.VMEM((4, rows, cols), BF),
            pltpu.VMEM((4, rows, cols), BF),
            pltpu.VMEM((rows, cols), BF),
            pltpu.VMEM((2, rows, cols), BF),
            DMA((6,)),
            DMA((6,)),
            DMA((4,)),
            DMA((4,)),
            DMA((4,)),
        ],
        compiler_params=params(cid),
    )(a)


def swap_kernel(a, out, ss, rs):
    p = place()
    peer = moved(p, z=2)
    greet((peer,))
    cp = put(a, out, ss, rs, peer)
    cp.start()
    cp.wait()


def swap(a, cid):
    return pl.pallas_call(
        swap_kernel,
        out_shape=jax.ShapeDtypeStruct(a.shape, a.dtype),
        in_specs=[ANY],
        out_specs=ANY,
        scratch_shapes=[DMA, DMA],
        compiler_params=params(cid),
    )(a)


def weights_kernel(wq, wo, wu, wd, oq, oo, ou, od, xs, xr, zs, zr, ls, bs, br):
    p = place()
    t = p["y"] * 2 + p["c"]
    me = p["x"] * 2 + p["zl"]
    xp = [moved(p, x=d) for d in STEPS]
    zp = [moved(p, z=1), moved(p, z=-1)]
    greet(tuple(xp + zp))
    half = (pl.ds(0, 128), pl.ds(128, 128))
    pieces = [(wq, 2048 * k + 256 * t, 256, oq, 256 * k) for k in range(3)]
    pieces += [(wu, 1024 * t, 1024, ou, 0), (wd, 1024 * t, 1024, od, 0)]
    outs = (oq, ou, od)

    def src(j):
        w, s, n, _, _ = pieces[j]
        return w.at[:, pl.ds(pl.multiple_of(s, 256), n)]

    def dst(j):
        _, _, n, o, at = pieces[j]
        return o.at[me, :, pl.ds(at, n)]

    own = [pltpu.make_async_copy(src(j), dst(j), ls.at[j]) for j in range(5)]
    for cp in own:
        cp.start()
    xcs = []
    for k in range(3):
        row = [put(src(j), dst(j), xs.at[k, j], xr.at[k, j], xp[k]) for j in range(5)]
        for cp in row:
            cp.start()
        xcs.append(row)
    holder = p["zl"] == p["c"]
    source = jnp.logical_and(holder, p["x"] == p["y"])
    bx = [put(wo, oo, bs.at[k], br.at[k], xp[k]) for k in range(3)]

    @pl.when(source)
    def _():
        for cp in bx:
            cp.start()
        cp = pltpu.make_async_copy(wo, oo, ls.at[5])
        cp.start()
        cp.wait()

    zcs = []

    def forward(n, i):
        for m in range(2):
            for j in range(3):
                ref = outs[j].at[i, half[m]]
                cp = put(ref, ref, zs.at[n, m, j], zr.at[n, m, j], zp[m])
                cp.start()
                zcs.append(cp)

    for cp in own:
        cp.wait()
    forward(0, me)
    for k, d in enumerate(STEPS):
        for cp in xcs[k]:
            cp.wait_recv()
        forward(k + 1, lax.rem(p["x"] - d + 4, 4) * 2 + p["zl"])
    bz = [put(oo.at[half[m]], oo.at[half[m]], bs.at[3 + m], br.at[3 + m], zp[m]) for m in range(2)]
    for k, d in enumerate(STEPS):

        @pl.when(jnp.logical_and(holder, lax.rem(p["x"] - d + 4, 4) == p["y"]))
        def _():
            bx[k].wait_recv()

    @pl.when(holder)
    def _():
        for cp in bz:
            cp.start()
        for cp in bz:
            cp.wait_send()

    @pl.when(jnp.logical_not(holder))
    def _():
        for cp in bz:
            cp.wait_recv()

    @pl.when(source)
    def _():
        for cp in bx:
            cp.wait_send()

    for cp in zcs:
        cp.wait_recv()
    for row in xcs:
        for cp in row:
            cp.wait_send()
    for cp in zcs:
        cp.wait_send()


def weights_gather(wq, wo, wu, wd, cid):
    s = jax.ShapeDtypeStruct
    return pl.pallas_call(
        weights_kernel,
        out_shape=(
            s((8, 256, 768), BF),
            s((256, 2048), BF),
            s((8, 256, 1024), BF),
            s((8, 256, 1024), BF),
        ),
        in_specs=[ANY] * 4,
        out_specs=(ANY,) * 4,
        scratch_shapes=[
            DMA((3, 5)),
            DMA((3, 5)),
            DMA((4, 2, 3)),
            DMA((4, 2, 3)),
            DMA((6,)),
            DMA((5,)),
            DMA((5,)),
        ],
        compiler_params=params(cid),
    )(wq, wo, wu, wd)


def grads_kernel(g, out, ma, mb, rx1, rz1, s1, s2, rx2, rz2, os, or_, ls):
    p = place()
    z = p["zh"] * 2 + p["zl"]
    w = g.shape[3] // 2
    ca, cb = pl.ds(0, w), pl.ds(w, w)
    xp = [moved(p, x=d) for d in STEPS]
    zp = [moved(p, z=d) for d in STEPS]
    greet(tuple(xp + zp))

    def rows_of(zz):
        return pl.ds(pl.multiple_of((zz // 2) * 128, 128), 128)

    ax, az = [], []
    for k, d in enumerate(STEPS):
        xx = lax.rem(p["x"] + d + 4, 4)
        zz = lax.rem(z + d + 4, 4)
        ax.append(put(g.at[xx, :, :, ca], rx1.at[k], os.at[0, k], or_.at[0, k], xp[k]))
        az.append(
            put(g.at[:, lax.rem(zz, 2), rows_of(zz), cb], rz1.at[k], os.at[1, k], or_.at[1, k], zp[k])
        )
    for k in range(3):
        ax[k].start()
        az[k].start()
    la = pltpu.make_async_copy(g.at[p["x"], :, :, ca], ma, ls.at[0])
    lb = pltpu.make_async_copy(g.at[:, p["zl"], rows_of(z), cb], mb, ls.at[1])
    la.start()
    lb.start()
    la.wait()
    lb.wait()
    for k in range(3):
        ax[k].wait_recv()
    for i in range(2):
        add_rows(s1.at[i], (0, 256), [(ma.at[i], 0)] + [(rx1.at[k, i], 0) for k in range(3)])
    bz = []
    for k, d in enumerate(STEPS):
        zz = lax.rem(z + d + 4, 4)
        cp = put(s1.at[lax.rem(zz, 2), rows_of(zz)], rz2.at[k], os.at[2, k], or_.at[2, k], zp[k])
        cp.start()
        bz.append(cp)
    for k in range(3):
        az[k].wait_recv()
    for i in range(4):
        add_rows(s2.at[i], (0, 128), [(mb.at[i], 0)] + [(rz1.at[k, i], 0) for k in range(3)])
    bx = []
    for k, d in enumerate(STEPS):
        xx = lax.rem(p["x"] + d + 4, 4)
        cp = put(s2.at[xx], rx2.at[k], os.at[3, k], or_.at[3, k], xp[k])
        cp.start()
        bx.append(cp)
    for cp in bz:
        cp.wait_recv()
    add_rows(
        out.at[:, ca],
        (0, 128),
        [(s1.at[p["zl"]], p["zh"] * 128)] + [(rz2.at[k], 0) for k in range(3)],
    )
    for cp in bx:
        cp.wait_recv()
    add_rows(out.at[:, cb], (0, 128), [(s2.at[p["x"]], 0)] + [(rx2.at[k], 0) for k in range(3)])
    for cp in ax + az + bx + bz:
        cp.wait_send()


def grads_reduce(g, cid):
    w = g.shape[-1]
    hw = w // 2
    g = g.reshape(4, 2, 256, w)
    v = pltpu.VMEM
    return pl.pallas_call(
        grads_kernel,
        out_shape=jax.ShapeDtypeStruct((128, w), BF),
        in_specs=[ANY],
        out_specs=pl.BlockSpec(memory_space=pltpu.VMEM),
        scratch_shapes=[
            v((2, 256, hw), BF),
            v((4, 128, hw), BF),
            v((3, 2, 256, hw), BF),
            v((3, 4, 128, hw), BF),
            v((2, 256, hw), BF),
            v((4, 128, hw), BF),
            v((3, 128, hw), BF),
            v((3, 128, hw), BF),
            DMA((4, 3)),
            DMA((4, 3)),
            DMA((2,)),
        ],
        compiler_params=params(cid),
    )(g)


def spread_kernel(a, out, os, or_, cs, cr, ls):
    p = place()
    c = p["c"]
    zh = p["zh"]
    yp = [moved(p, y=d) for d in STEPS]
    far, twin = moved(p, z=2), moved(p, c=1)
    greet(tuple(yp + [far, twin]))
    lo, hi = pl.ds(0, 64), pl.ds(64, 64)

    def block(d):
        return lax.rem(p["y"] + d + 4, 4) * 2 + c

    own = pltpu.make_async_copy(a, out.at[zh, block(0)], ls)
    own.start()
    sends = []
    twins = []

    def send(src, at, n, to):
        cp = put(src, out.at[at], os.at[n], or_.at[n], to)
        cp.start()
        sends.append(cp)
        return cp

    def share(src, at):
        n = len(twins)
        cp = put(src, out.at[at], cs.at[n], cr.at[n], twin)
        cp.start()
        twins.append(cp)

    me_lo, me_hi = (zh, block(0), lo), (zh, block(0), hi)
    first = [send(a.at[lo], me_lo, k, yp[k]) for k in range(3)]
    cross = send(a.at[hi], me_hi, 3, far)
    firstz = [send(a.at[lo], me_lo, 4, far)]
    second = [send(a.at[hi], me_hi, 5 + k, yp[k]) for k in range(3)]
    share(a.at[lo], me_lo)
    share(a.at[hi], me_hi)
    for k, d in enumerate(STEPS):
        first[k].wait_recv()
        at = (zh, block(-d), lo)
        firstz.append(send(out.at[at], at, 8 + k, far))
        share(out.at[at], at)
    cross.wait_recv()
    at = (1 - zh, block(0), hi)
    third = [send(out.at[at], at, 11 + k, yp[k]) for k in range(3)]
    share(out.at[at], at)
    for k, d in enumerate(STEPS):
        second[k].wait_recv()
        at = (zh, block(-d), hi)
        share(out.at[at], at)
    for k, d in enumerate((0,) + STEPS):
        firstz[k].wait_recv()
        at = (1 - zh, block(-d), lo)
        share(out.at[at], at)
    for k, d in enumerate(STEPS):
        third[k].wait_recv()
        at = (1 - zh, block(-d), hi)
        share(out.at[at], at)
    for cp in twins:
        cp.wait_recv()
    for cp in twins + sends:
        cp.wait_send()
    own.wait()


def spread(a, cid):
    return pl.pallas_call(
        spread_kernel,
        out_shape=jax.ShapeDtypeStruct((2, 8) + a.shape, a.dtype),
        in_specs=[ANY],
        out_specs=ANY,
        scratch_shapes=[DMA((14,)), DMA((14,)), DMA((16,)), DMA((16,)), DMA],
        compiler_params=params(cid),
    )(a)


def small_kernel(v, out, bx, bz, bc, by, os, or_):
    p = place()
    z = p["zh"] * 2 + p["zl"]
    xp = [moved(p, x=d) for d in STEPS]
    zp = [moved(p, z=d) for d in STEPS]
    yp = [moved(p, y=d) for d in STEPS]
    twin = moved(p, c=1)
    greet(tuple(xp + zp + yp + [twin]))
    sends = []

    def exchange(buf, at, peers, n):
        cps = [put(buf.at[at], buf.at[at], os.at[n + k], or_.at[n + k], q) for k, q in enumerate(peers)]
        for cp in cps:
            cp.start()
        for cp in cps:
            cp.wait_recv()
        sends.extend(cps)

    bx[p["x"]] = v[...]
    exchange(bx, p["x"], xp, 0)
    bz[z] = bx[0] + bx[1] + bx[2] + bx[3]
    exchange(bz, z, zp, 3)
    bc[p["c"]] = bz[0] + bz[1] + bz[2] + bz[3]
    exchange(bc, p["c"], [twin], 6)
    by[p["y"], 0:96] = bc[0, 0:96] + bc[1, 0:96]
    by[p["y"], 96:112] = bc[0, 96:112]
    by[p["y"], 112:128] = bc[1, 96:112]
    exchange(by, p["y"], yp, 7)
    out[...] = by[...]
    for cp in sends:
        cp.wait_send()


def small_sums(v, cid):
    vm = pltpu.VMEM
    spec = pl.BlockSpec(memory_space=pltpu.VMEM)
    return pl.pallas_call(
        small_kernel,
        out_shape=jax.ShapeDtypeStruct((4, 128, 128), F32),
        in_specs=[spec],
        out_specs=spec,
        scratch_shapes=[
            vm((4, 112, 128), F32),
            vm((4, 112, 128), F32),
            vm((2, 112, 128), F32),
            vm((4, 128, 128), F32),
            DMA((10,)),
            DMA((10,)),
        ],
        compiler_params=params(cid),
    )(v)


def norm_rows(values, gain, shift):
    average = jnp.mean(values, axis=-1, keepdims=True)
    centred = values - average
    variance = jnp.mean(centred * centred, axis=-1, keepdims=True)
    return centred * lax.rsqrt(variance + epsilon) * gain + shift


def gelu_tanh(values):
    return jax.nn.gelu(values, approximate=True)


def half_layout(lengths_row, zh):
    rows = jnp.arange(1024, dtype=jnp.int32)
    block = rows // 128
    local = rows % 128
    device = (block // 2) * 4 + zh * 2 + block % 2
    is_prompt = local < 64
    flat = device * 64 + jnp.where(is_prompt, local, local - 64)
    continuation = jnp.where(is_prompt, -1, flat // CONT)
    inner = jnp.where(is_prompt, flat, flat % CONT)
    prompt_len = lengths_row[0]
    own_len = jnp.where(
        is_prompt, prompt_len, jnp.take(lengths_row, 1 + jnp.maximum(continuation, 0))
    )
    position = jnp.where(is_prompt, inner, prompt_len + inner)
    return (continuation, inner, position, inner < own_len)


def allowed_pairs(cont_query, inner_query, cont_key, inner_key, live_key):
    prompt_key = cont_key[None, :] < 0
    earlier = inner_key[None, :] <= inner_query[:, None]
    from_prompt = prompt_key & ((cont_query[:, None] >= 0) | earlier)
    same_cont = ~prompt_key & (cont_key[None, :] == cont_query[:, None]) & earlier
    return live_key[None, :] & (from_prompt | same_cont)


def dot(a, b):
    return jnp.dot(a, b, preferred_element_type=F32)


def dot_t(a, b):
    return lax.dot_general(a, b, (((1,), (1,)), ((), ())), preferred_element_type=F32)


def t_dot(a, b):
    return lax.dot_general(a, b, (((0,), (0,)), ((), ())), preferred_element_type=F32)


def body(
    tokens,
    cotangent,
    lengths,
    qkv_weight,
    out_weight,
    up_weight,
    down_weight,
    bias_query,
    bias_value,
    out_bias,
    up_bias,
    down_bias,
    norm_gain_one,
    norm_shift_one,
    norm_gain_two,
    norm_shift_two,
):
    p = place()
    t = p["y"] * 2 + p["c"]
    zh = p["zh"]
    scale = HEAD ** (-0.5)
    out_b = out_bias.astype(F32)
    down_b = down_bias.astype(F32)
    gain_one = norm_gain_one.astype(F32)
    shift_one = norm_shift_one.astype(F32)
    gain_two = norm_gain_two.astype(F32)
    shift_two = norm_shift_two.astype(F32)

    def cut(v, n):
        return lax.dynamic_slice_in_dim(v, t * n, n, v.ndim - 1)

    tok = tokens.astype(F32)
    w_qkv, w_out, w_up, w_down = weights_gather(qkv_weight, out_weight, up_weight, down_weight, 0)
    w_qkv = w_qkv.reshape(2048, 768)
    w_up = w_up.reshape(2048, 1024)
    w_down = w_down.reshape(2048, 1024)
    normed, norm_one_back = jax.vjp(norm_rows, tok, gain_one, shift_one)
    n1 = team_gather(normed.astype(BF), 1).reshape(1024, 2048)
    dy = team_gather(cotangent, 2).reshape(1024, 2048)
    qb = cut(bias_query, 256).astype(F32)
    vb = cut(bias_value, 256).astype(F32)
    bias_cat = jnp.concatenate([qb, jnp.zeros_like(qb), vb])
    mixed = (dot(n1, w_qkv) + bias_cat).astype(BF)
    far = swap(mixed[:, 256:], 3)
    q = mixed[:, :256].reshape(1024, 2, HEAD)
    k = jnp.concatenate([mixed[:, 256:512], far[:, :256]]).reshape(2048, 2, HEAD)
    v = jnp.concatenate([mixed[:, 512:], far[:, 256:]]).reshape(2048, 2, HEAD)
    lq = half_layout(lengths[0], zh)
    lk = [jnp.concatenate([a, b]) for a, b in zip(lq, half_layout(lengths[0], 1 - zh))]
    slopes = jnp.exp2(-8.0 * (t * 2 + jnp.arange(2, dtype=jnp.int32) + 1).astype(F32) / H)
    s = jnp.einsum("qhd,khd->hqk", q, k, preferred_element_type=F32) * scale
    distance = (lq[2][:, None] - lk[2][None, :]).astype(F32)
    s = s - slopes[:, None, None] * distance[None]
    mask = allowed_pairs(lq[0], lq[1], lk[0], lk[1], lk[3])
    s = jnp.where(mask[None], s, -1e30)
    top = jnp.max(s, axis=-1, keepdims=True)
    log_total = top + jnp.log(jnp.sum(jnp.exp(s - top), axis=-1, keepdims=True))
    probs = jnp.exp(s - log_total)
    heads = jnp.einsum("hqk,khd->qhd", probs.astype(BF), v, preferred_element_type=F32)
    heads = heads.astype(BF).reshape(1024, 256)

    attended = team_reduce(dot(heads, w_out).astype(BF).reshape(8, 128, 2048), 4)
    middle = tok + attended + out_b
    normed_two, norm_two_back = jax.vjp(norm_rows, middle, gain_two, shift_two)
    n2 = team_gather(normed_two.astype(BF), 5).reshape(1024, 2048)
    hidden = dot(n2, w_up) + cut(up_bias, 1024).astype(F32)
    activated, gelu_back = jax.vjp(gelu_tanh, hidden)
    act = activated.astype(BF)
    branch = team_reduce(dot_t(act, w_down).astype(BF).reshape(8, 128, 2048), 6)
    output = (middle + branch + down_b).astype(BF)
    (pre_grad,) = gelu_back(dot(dy, w_down))
    dpre = pre_grad.astype(BF)
    dn2 = team_reduce(dot_t(dpre, w_up).astype(BF).reshape(8, 128, 2048), 7)
    mid_norm, gain_two_grad, shift_two_grad = norm_two_back(dn2)
    dmiddle = cotangent.astype(F32) + mid_norm
    dattn_own = dmiddle.astype(BF)
    dattn = team_gather(dattn_own, 8).reshape(1024, 2048)
    dheads = dot_t(dattn, w_out).astype(BF).reshape(1024, 2, HEAD)

    probs_low = probs.astype(BF)
    dv = jnp.einsum("hqk,qhd->khd", probs_low, dheads, preferred_element_type=F32)
    dprobs = jnp.einsum("qhd,khd->hqk", dheads, v, preferred_element_type=F32)
    inner_sum = jnp.sum(probs * dprobs, axis=-1, keepdims=True)
    ds = (probs * (dprobs - inner_sum)).astype(BF)
    dq = jnp.einsum("hqk,khd->qhd", ds, k, preferred_element_type=F32) * scale
    dk = jnp.einsum("hqk,qhd->khd", ds, q, preferred_element_type=F32) * scale
    dkv = jnp.concatenate([dk.reshape(2048, 256), dv.reshape(2048, 256)], axis=1)
    dkv = dkv[:1024] + swap(dkv[1024:].astype(BF), 9).astype(F32)
    dqkv = jnp.concatenate([dq.reshape(1024, 256), dkv], axis=1).astype(BF)
    dn1 = team_reduce(dot_t(dqkv, w_qkv).astype(BF).reshape(8, 128, 2048), 10)
    token_norm, gain_one_grad, shift_one_grad = norm_one_back(dn1)
    input_grad = (dmiddle + token_norm).astype(BF)
    heads_all = team_gather(heads.reshape(8, 128, 256).reshape(1024, 256), 11)
    heads_all = heads_all.transpose(1, 0, 2).reshape(1024, 2048)
    g = jnp.concatenate(
        [
            t_dot(n1, dqkv).astype(BF),
            t_dot(heads_all, cut(dattn, 256)).astype(BF),
            t_dot(n2, dpre).astype(BF),
            t_dot(dy, act).astype(BF),
        ],
        axis=1,
    )
    g = spread(grads_reduce(g, 12), 13).astype(F32)

    def full(part):
        return part.transpose(0, 2, 1, 3).reshape(256, -1)

    qkv_grad = jnp.concatenate([full(g[..., 256 * i : 256 * i + 256]) for i in range(3)], axis=1)

    def total(v):
        return jnp.sum(v.astype(F32), axis=0)

    rows = jnp.concatenate(
        [
            total(dattn_own),
            total(cotangent),
            gain_one_grad,
            shift_one_grad,
            gain_two_grad,
            shift_two_grad,
        ]
    ).reshape(96, 128)
    dqkv_sum = total(dqkv)
    cols = jnp.concatenate(
        [total(dpre), dqkv_sum[:256], dqkv_sum[512:], jnp.zeros((512,), F32)]
    ).reshape(16, 128)
    sums = small_sums(jnp.concatenate([rows, cols]), 14)
    rows = (sums[0, :96] + sums[1, :96] + sums[2, :96] + sums[3, :96]).reshape(6, 2048)
    cols = sums[:, 96:].reshape(8, 2048)
    return (
        output,
        input_grad,
        qkv_grad,
        full(g[..., 768:1024]),
        full(g[..., 1024:2048]),
        full(g[..., 2048:]),
        cols[:, 1024:1280].reshape(2048),
        cols[:, 1280:1536].reshape(2048),
        rows[0],
        cols[:, :1024].reshape(8192),
        rows[1],
        rows[2],
        rows[3],
        rows[4],
        rows[5],
    )


def solution(mesh):
    fine = Mesh(mesh.devices.reshape(4, 2, 4, 2, 2), AXES)
    tok = P(AXES, None)
    row = P(("x", "zl"), None)
    in_specs = (tok, tok, row, row, row, row, row) + (P(),) * 9
    out_specs = (tok, tok, row, row, row, row) + (P(),) * 9
    return jax.shard_map(body, mesh=fine, in_specs=in_specs, out_specs=out_specs, check_vma=False)
```

time: 4570 us -> 904 us (0.20)
  waiting for transfers between devices: 4130 us -> 0 us
  Pallas kernels: 0 us -> 568 us
  matrix products: 208 us -> 111 us
  local copies, waits for them, and re-layouts: 58.5 us -> 107 us
    all_gather x4 -> x0, waiting for transfers between devices: 1840 us -> none  [the longest x1 642 us: body(): lax.all_gather(down_weight, 'dp', axis=0, tiled=True)]
    reduce_scatter x2 -> x0, waiting for transfers between devices: 1840 us -> none  [the longest x1 1270 us: body(): lax.psum_scatter(jnp.concatenate([contract_rows(normed_two_low, pre_low),...]
    pallas_call x0 -> x15, Pallas kernels: none -> 568 us  [the longest x5 127 us: team_gather(): pl.pallas_call(team_gather_kernel, out_shape=jax.ShapeDtypeStruct((8,) +...]
    psum x2 -> x0, waiting for transfers between devices: 381 us -> none  [the longest x1 248 us: body(): lax.psum(attn_part, 'seq').astype(jnp.float32)]
    dot_general x40 -> x18, matrix products: 208 us -> 111 us  [the longest x4 25.7 us: dot(): return jnp.dot(a, b, preferred_element_type=F32)]
    all_to_all x4 -> x0, waiting for transfers between devices: 68.8 us -> none  [the longest x1 21.9 us: body(): lax.all_to_all(mixed.reshape(per_device, 3, H, HEAD), 'seq', split_axis=2...]
  transfers between devices with their start and end apart: 12 -> 0, of which waited for: 12 -> 0; matrix products, arithmetic and copies ran while one was open for 4% -> 0% of each run, Pallas kernels for 0% -> 0%
where the time goes in v1:
time: 904 us; the launch traced here: 894 us
  Pallas kernels  568 us (63%)
  matrix products  111 us (12%)
  local copies, waits for them, and re-layouts  107 us (12%)
  other arithmetic  106 us (12%)
    pallas_call x5, Pallas kernels, team_gather(): pl.pallas_call(team_gather_kernel, out_shape=jax.ShapeDtypeStruct((8,) +...  127 us
    pallas_call x1, Pallas kernels, weights_gather(): pl.pallas_call(weights_kernel, out_shape=(s((8, 256, 768), BF), s((256, 2...  122 us
    pallas_call x4, Pallas kernels, team_reduce(): pl.pallas_call(team_reduce_kernel, out_shape=jax.ShapeDtypeStruct((rows,...  99.2 us
    pallas_call x1, Pallas kernels, grads_reduce(): pl.pallas_call(grads_kernel, out_shape=jax.ShapeDtypeStruct((128, w), BF)...  91.9 us
    pallas_call x1, Pallas kernels, spread(): pl.pallas_call(spread_kernel, out_shape=jax.ShapeDtypeStruct((2, 8) + a.s...  57.7 us
    pallas_call x2, Pallas kernels, swap(): pl.pallas_call(swap_kernel, out_shape=jax.ShapeDtypeStruct(a.shape, a.dty...  51.5 us
    transpose x8, local copies, waits for them, and re-layouts, full(): return part.transpose(0, 2, 1, 3).reshape(256, -1)  35.7 us
    unnamed x113, local copies, waits for them, and re-layouts  31.1 us

profile of v1, /device:TPU:1, one launch (start us, length us, event | category | flops | bytes accessed | tf_op | source)
XLA Modules:
  0.0 894.3 jit_solution(4646631348121927774)
XLA Ops:
  5.5 3.9 fusion.54
  19.7 4.0 fusion.3
  23.7 26.4 %shard_map.271 = bf16[8,128,2048]{2,1,0:T(8,128)(2,1)} custom-call(bf16[128,2048]{1,0:T(8,128)(2,1)} %fusion.33.a), custom_call_target="tpu_custom_call" | custom-call | tf_op jit(solution)/shard_map/pallas_call | solution.py:115
  50.0 25.2 %shard_map.277 = bf16[8,128,2048]{2,1,0:T(8,128)(2,1)} custom-call(bf16[128,2048]{1,0:T(8,128)(2,1)} %a.1), custom_call_target="tpu_custom_call" | custom-call | tf_op jit(solution)/shard_map/pallas_call | solution.py:115
  75.2 4.0 subtract_convert_fusion
  79.2 121.8 %shard_map.272 = (bf16[8,256,768]{2,1,0:T(8,128)(2,1)}, bf16[256,2048]{1,0:T(8,128)(2,1)}, bf16[8,256,1024]{2,1,0:T(8,128)(2,1)}, bf16[8,256,1024]{2,1,0:T(8,128)(2,1)}) custom-call(bf16[256,6144]{1,0:T(8,128)(2,1)} %wq.1, bf16[256,2048]{1,0:T(8,128)(2,1)} %wo.1, bf16[256,8192]{1,0:T(8,128)(2,1)} %wu.1, bf16[256,8192]{1,0:T(8,128)(2,1)} %wd.1), custom_call_target="tpu_custom_call" | custom-call | tf_op jit(solution)/shard_map/pallas_call | solution.py:330
  201.0 6.6 add_convert_fusion
  208.6 25.0 %shard_map.273 = bf16[1024,512]{1,0:T(8,128)(2,1)} custom-call(bf16[1024,512]{1,0:T(8,128)(2,1)} %slice.162.a), custom_call_target="tpu_custom_call" | custom-call | tf_op jit(solution)/shard_map/pallas_call | solution.py:227
  241.2 11.2 %fusion.83 = (f32[2,1024]{1,0:T(2,128)S(1)}, f32[2,1024,2048]{2,1,0:T(8,128)}) fusion(f32[1024,2048]{1,0:T(8,128)} %subtract_convert_fusion, f32[2]{0:T(128)S(1)} %multiply_exponential_fusion, bf16[1024,2,128]{0,2,1:T(8,128)(2,1)S(1)} %bitcast.172, bf16[2048,2,128]{0,2,1:T(8,128)(2,1)} %bitcast.174, pred[1024,2048]{1,0:T(8,128)(4,1)S(1)} %fusion.3), kind=kOutput, calls=%fused_computation.202 | convolution fusion | flops 1094711296 | bytes 28844040 | tf_op jit(solution)/shard_map/qhd,khd->hqk/dot_general | solution.py:670
  252.4 8.2 exponential_reduce_fusion
  260.6 8.8 fusion.27
  270.4 3.3 convolution_convert_fusion
  273.8 24.0 %shard_map.274 = f32[128,2048]{1,0:T(8,128)} custom-call(bf16[8,128,2048]{2,1,0:T(8,128)(2,1)} %bitcast.169), custom_call_target="tpu_custom_call" | custom-call | tf_op jit(solution)/shard_map/pallas_call | solution.py:196
  300.6 25.9 %shard_map.275 = bf16[8,128,2048]{2,1,0:T(8,128)(2,1)} custom-call(bf16[128,2048]{1,0:T(8,128)(2,1)} %add_convert_fusion.3.a), custom_call_target="tpu_custom_call" | custom-call | tf_op jit(solution)/shard_map/pallas_call | solution.py:115
  326.5 24.6 %shard_map.282 = bf16[8,1024,256]{2,1,0:T(8,128)(2,1)} custom-call(bf16[1024,256]{1,0:T(8,128)(2,1)} %copy.66.a), custom_call_target="tpu_custom_call" | custom-call | tf_op jit(solution)/shard_map/pallas_call | solution.py:115
  351.1 6.5 copy.56
  357.6 7.7 fusion.84
  365.3 8.2 convert_reduce_fusion
  373.5 6.4 convolution_convert_fusion.2
  379.9 6.1 convolution_convert_fusion.3
  386.0 24.2 %shard_map.278 = f32[128,2048]{1,0:T(8,128)} custom-call(bf16[8,128,2048]{2,1,0:T(8,128)(2,1)} %bitcast.190), custom_call_target="tpu_custom_call" | custom-call | tf_op jit(solution)/shard_map/pallas_call | solution.py:196
  410.2 9.8 %convert_bitcast_fusion = bf16[2048,1024]{0,1:T(8,128)(2,1)} fusion(bf16[1024,2048]{1,0:T(8,128)(2,1)S(1)} %bitcast.194, f32[1024,1024]{1,0:T(8,128)} %copy-done.46, f32[1024]{0:T(1024)S(1)} %dynamic-slice_convert_fusion), kind=kOutput, calls=%fused_computation.33 | convolution fusion | flops 4307550208 | bytes 12587008 | tf_op jit(solution)/shard_map/dot_general | solution.py:616
  419.9 7.1 convolution_convert_fusion.4
  427.1 24.8 %shard_map.276 = f32[128,2048]{1,0:T(8,128)} custom-call(bf16[8,128,2048]{2,1,0:T(8,128)(2,1)} %bitcast.189), custom_call_target="tpu_custom_call" | custom-call | tf_op jit(solution)/shard_map/pallas_call | solution.py:196
  456.9 24.8 %shard_map.279 = bf16[8,128,2048]{2,1,0:T(8,128)(2,1)} custom-call(bf16[128,2048]{1,0:T(8,128)(2,1)} %get-tuple-element.32.a), custom_call_target="tpu_custom_call" | custom-call | tf_op jit(solution)/shard_map/pallas_call | solution.py:115
  481.8 3.5 convolution_convert_fusion.6
  486.5 7.6 fusion.14
  495.9 9.2 %multiply_reduce_fusion = (f32[2,1024]{1,0:T(2,128)}, f32[2,1024,2048]{2,1,0:T(8,128)S(1)}) fusion(f32[2,1024,2048]{2,1,0:T(8,128)} %get-tuple-element.69, f32[2,1024]{1,0:T(2,128)S(1)} %log_add_fusion, bf16[1024,2,128]{0,2,1:T(8,128)(2,1)} %bitcast.201, bf16[1024,256]{1,0:T(8,128)(2,1)} %get-tuple-element.49, bf16[1024,256]{1,0:T(8,128)(2,1)S(1)} %get-tuple-element.45), kind=kOutput, calls=%fused_computation.1 | convolution fusion | flops 1088419840 | bytes 35143680 | tf_op jit(solution)/shard_map/qhd,khd->hqk/dot_general | solution.py:701
  505.1 8.3 multiply_convert_fusion
  519.0 3.0 copy.68
  525.5 26.5 %shard_map.280 = bf16[1024,512]{1,0:T(8,128)(2,1)} custom-call(bf16[1024,512]{1,0:T(8,128)(2,1)} %fusion.21.a), custom_call_target="tpu_custom_call" | custom-call | tf_op jit(solution)/shard_map/pallas_call | solution.py:227
  554.5 3.9 convolution_convert_fusion.5
  558.4 27.4 %pad_maximum_fusion = bf16[2048,3072]{0,1:T(8,128)(2,1)} fusion(bf16[2048,1024]{0,1:T(8,128)(2,1)S(1)} %copy-done.18, bf16[2048,1024]{0,1:T(8,128)(2,1)S(1)} %copy-done.17, bf16[2048,256]{0,1:T(8,128)(2,1)S(1)} %copy-done.22, bf16[2048,768]{0,1:T(8,128)(2,1)S(1)} %convolution_convert_fusion.5), kind=kLoop, calls=%fused_computation.6 | loop fusion | flops 50331648 | bytes 25165824 | tf_op jit(solution)/shard_map/concatenate | solution.py:714
  585.8 16.6 %copy.57 = bf16[2048,3072]{1,0:T(8,128)(2,1)} copy(bf16[2048,3072]{0,1:T(8,128)(2,1)} %pad_maximum_fusion) | data formatting | bytes 25165824 | tf_op jit(solution)/shard_map/concatenate | solution.py:714
  602.4 91.9 %shard_map.283.a = bf16[128,3072]{1,0:T(8,128)(2,1)} custom-call(bf16[4,2,256,3072]{3,2,1,0:T(8,128)(2,1)} %bitcast.166), custom_call_target="tpu_custom_call" | custom-call | tf_op jit(solution)/shard_map/pallas_call | solution.py:421
  694.6 5.0 convolution_convert_fusion.1
  699.7 26.2 %shard_map.281 = f32[128,2048]{1,0:T(8,128)} custom-call(bf16[8,128,2048]{2,1,0:T(8,128)(2,1)} %bitcast.188), custom_call_target="tpu_custom_call" | custom-call | tf_op jit(solution)/shard_map/pallas_call | solution.py:196
  732.7 18.9 %shard_map.285 = f32[4,128,128]{2,1,0:T(8,128)} custom-call(f32[112,128]{1,0:T(8,128)} %copy-done.29), custom_call_target="tpu_custom_call" | custom-call | tf_op jit(solution)/shard_map/pallas_call | solution.py:554
  755.8 57.7 %shard_map.284 = bf16[2,8,128,3072]{3,2,1,0:T(8,128)(2,1)} custom-call(bf16[128,3072]{1,0:T(8,128)(2,1)} %shard_map.283.a), custom_call_target="tpu_custom_call" | custom-call | tf_op jit(solution)/shard_map/pallas_call | solution.py:508
  813.5 14.5 %convert_element_type.168 = f32[2,8,128,3072]{3,2,1,0:T(8,128)} convert(bf16[2,8,128,3072]{3,2,1,0:T(8,128)(2,1)} %shard_map.284) | non-fusion elementwise | flops 6291456 | bytes 37748736 | tf_op jit(solution)/shard_map/convert_element_type | solution.py:723
  828.0 6.3 slice_bitcast_fusion.2
  834.3 9.5 %slice_bitcast_fusion = (f32[2,128,8,1024]{3,1,2,0:T(8,128)}, f32[2,128,8,1024]{3,1,2,0:T(8,128)S(1)}) fusion(f32[2,8,128,3072]{3,2,1,0:T(8,128)} %convert_element_type.168), kind=kLoop, calls=%fused_computation.9 | loop fusion | bytes 33554432 | tf_op jit(solution)/shard_map/transpose | solution.py:726
  843.8 8.2 copy.63
  852.0 11.2 %copy.78 = f32[32,8,8,1024]{3,1,2,0:T(8,128)} copy(f32[32,8,8,1024]{3,2,1,0:T(8,128)S(1)} %bitcast.167) | data formatting | bytes 16777216
  863.2 3.0 copy.61
  874.7 3.1 pad_maximum_fusion.1
  877.8 5.1 copy.62
  882.9 11.0 %copy.77 = f32[32,8,8,1024]{3,1,2,0:T(8,128)} copy(f32[32,8,8,1024]{3,2,1,0:T(8,128)S(1)} %bitcast.168) | data formatting | bytes 16777216
  (178 shorter events, 66.7 us)
Async XLA Ops:
  1.9 15.6 %copy-start.35 = (f32[128]{0:T(128)}, f32[128]{0:T(128)S(1)}, u32[]{:S(2)}) copy-start(f32[128]{0:T(128)S(1)} %broadcast_multiply_fusion.1) | copy-start | bytes 1540
  3.2 14.2 %copy-start.40 = (f32[128]{0:T(128)}, f32[128]{0:T(128)S(1)}, u32[]{:S(2)}) copy-start(f32[128]{0:T(128)S(1)} %fusion.35) | copy-start | bytes 1540
  3.2 14.2 %copy-start.37 = (f32[128]{0:T(128)}, f32[128]{0:T(128)S(1)}, u32[]{:S(2)}) copy-start(f32[128]{0:T(128)S(1)} %fusion.68) | copy-start | bytes 1540
  10.8 6.6 copy-start.25
  252.4 8.2 copy-start.9
  260.6 9.8 %copy-start.23 = (bf16[256,2048]{1,0:T(8,128)(2,1)S(1)}, bf16[256,2048]{1,0:T(8,128)(2,1)}, u32[]{:S(2)}) copy-start(bf16[256,2048]{1,0:T(8,128)(2,1)} %get-tuple-element.21) | copy-start | bytes 3145732
  273.7 24.1 %copy-start = (bf16[128,2048]{1,0:T(8,128)(2,1)S(1)}, bf16[128,2048]{1,0:T(8,128)(2,1)}, u32[]{:S(2)}) copy-start(bf16[128,2048]{1,0:T(8,128)(2,1)} %param.18) | copy-start | bytes 1572868
  273.7 24.1 %copy-start.34 = (f32[2048]{0:T(1024)S(1)}, f32[2048]{0:T(1024)}, u32[]{:S(2)}) copy-start(f32[2048]{0:T(1024)} %convert_element_type.145) | copy-start | bytes 24580
  273.7 25.8 %copy-start.27 = (f32[2048]{0:T(1024)S(1)}, f32[2048]{0:T(1024)}, u32[]{:S(2)}) copy-start(f32[2048]{0:T(1024)} %convert_element_type.146) | copy-start | bytes 24580
  273.7 25.8 %copy-start.33 = (f32[2048]{0:T(1024)S(1)}, f32[2048]{0:T(1024)}, u32[]{:S(2)}) copy-start(f32[2048]{0:T(1024)} %convert_element_type.147) | copy-start | bytes 24580
  357.6 7.7 copy-start.13
  357.6 7.7 copy-start.42
  365.2 8.2 copy-start.46
  365.3 8.2 copy-start.14
  373.5 6.4 copy-start.44
  410.2 9.8 %copy-start.43 = (bf16[8,256,1024]{2,1,0:T(8,128)(2,1)S(1)}, bf16[8,256,1024]{2,1,0:T(8,128)(2,1)}, u32[]{:S(2)}) copy-start(bf16[8,256,1024]{2,1,0:T(8,128)(2,1)} %get-tuple-element.23) | copy-start | bytes 12582916
  410.2 9.8 %copy-start.47 = (f32[1024,1024]{1,0:T(8,128)S(1)}, f32[1024,1024]{1,0:T(8,128)}, u32[]{:S(2)}) copy-start(f32[1024,1024]{1,0:T(8,128)} %copy-done.46) | copy-start | bytes 12582916
  427.1 24.8 %copy-start.7 = (f32[128,2048]{1,0:T(8,128)S(1)}, f32[128,2048]{1,0:T(8,128)}, u32[]{:S(2)}) copy-start(f32[128,2048]{1,0:T(8,128)} %shard_map.278) | copy-start | bytes 3145732
  427.1 25.8 %copy-start.30 = (f32[2048]{0:T(1024)S(1)}, f32[2048]{0:T(1024)}, u32[]{:S(2)}) copy-start(f32[2048]{0:T(1024)} %convert_element_type.152) | copy-start | bytes 24580
  451.9 3.4 copy-start.10
  455.3 30.0 %copy-start.5 = (f32[128,2048]{1,0:T(8,128)}, f32[128,2048]{1,0:T(8,128)S(1)}, u32[]{:S(2)}) copy-start(f32[128,2048]{1,0:T(8,128)S(1)} %get-tuple-element.34) | copy-start | bytes 3145732
  455.3 26.5 %copy-start.16 = (bf16[1024,8,256]{0,2,1:T(8,128)(2,1)S(1)}, bf16[1024,8,256]{0,2,1:T(8,128)(2,1)}, u32[]{:S(2)}) copy-start(bf16[1024,8,256]{0,2,1:T(8,128)(2,1)} %copy.56) | copy-start | bytes 12582916
  481.7 3.5 copy-start.15
  481.7 3.5 copy-start.24
  486.5 7.6 copy-start.19
  505.1 8.3 copy-start.4
  519.0 4.0 copy-start.2
  523.0 28.9 %copy-start.3 = (f32[2048,256]{1,0:T(8,128)S(1)}, f32[2048,256]{1,0:T(8,128)}, u32[]{:S(2)}) copy-start(f32[2048,256]{1,0:T(8,128)} %copy.68) | copy-start | bytes 6291460
  525.5 28.1 %copy-start.20 = (bf16[1024,256]{1,0:T(8,128)(2,1)S(1)}, bf16[1024,256]{1,0:T(8,128)(2,1)}, u32[]{:S(2)}) copy-start(bf16[1024,256]{1,0:T(8,128)(2,1)} %copy.67) | copy-start | bytes 1572868
  552.0 2.5 copy-start.12
  554.5 3.9 copy-start.17
  554.5 3.9 copy-start.18
  554.5 3.9 copy-start.22
  602.4 91.9 %copy-start.21 = (bf16[1024,256]{1,0:T(8,128)(2,1)S(1)}, bf16[1024,256]{1,0:T(8,128)(2,1)}, u32[]{:S(2)}) copy-start(bf16[1024,256]{1,0:T(8,128)(2,1)} %copy.67) | copy-start | bytes 1572868
  602.4 92.2 %copy-start.45 = (bf16[8,256,768]{2,1,0:T(8,128)(2,1)S(1)}, bf16[8,256,768]{2,1,0:T(8,128)(2,1)}, u32[]{:S(2)}) copy-start(bf16[8,256,768]{2,1,0:T(8,128)(2,1)} %get-tuple-element.20) | copy-start | bytes 9437188
  699.6 26.3 %copy-start.1 = (bf16[128,2048]{1,0:T(8,128)(2,1)S(1)}, bf16[128,2048]{1,0:T(8,128)(2,1)}, u32[]{:S(2)}) copy-start(bf16[128,2048]{1,0:T(8,128)(2,1)} %param.18) | copy-start | bytes 1572868
  699.6 26.3 %copy-start.26 = (f32[2048]{0:T(1024)S(1)}, f32[2048]{0:T(1024)}, u32[]{:S(2)}) copy-start(f32[2048]{0:T(1024)} %copy-done.25) | copy-start | bytes 24580
  699.6 26.3 %copy-start.36 = (f32[128]{0:T(128)S(1)}, f32[128]{0:T(128)}, u32[]{:S(2)}) copy-start(f32[128]{0:T(128)} %copy-done.35) | copy-start | bytes 1540
  699.6 27.9 %copy-start.41 = (f32[128]{0:T(128)S(1)}, f32[128]{0:T(128)}, u32[]{:S(2)}) copy-start(f32[128]{0:T(128)} %copy-done.40) | copy-start | bytes 1540
  699.6 27.9 %copy-start.38 = (f32[128]{0:T(128)S(1)}, f32[128]{0:T(128)}, u32[]{:S(2)}) copy-start(f32[128]{0:T(128)} %copy-done.37) | copy-start | bytes 1540
  699.6 29.7 %copy-start.6 = (f32[128,2048]{1,0:T(8,128)S(1)}, f32[128,2048]{1,0:T(8,128)}, u32[]{:S(2)}) copy-start(f32[128,2048]{1,0:T(8,128)} %copy-done.5) | copy-start | bytes 3145732
  699.6 29.7 %copy-start.11 = (bf16[128,2048]{1,0:T(8,128)(2,1)S(1)}, bf16[128,2048]{1,0:T(8,128)(2,1)}, u32[]{:S(2)}) copy-start(bf16[128,2048]{1,0:T(8,128)(2,1)} %a.1) | copy-start | bytes 1572868
  725.9 6.0 copy-start.28
  725.9 6.1 copy-start.32
  725.9 6.1 copy-start.31
  725.9 6.1 copy-start.39
  732.0 0.6 copy-start.29
  863.2 5.2 copy-start.8

commit v2 on v0

v2 whole, which is shorter than its diff:
```python
import functools

import jax
import jax.numpy as jnp
from jax import lax
from jax.experimental import pallas as pl
from jax.experimental.pallas import tpu as pltpu
from jax.sharding import Mesh, PartitionSpec as P

H = 16
HEAD = 128
AXES = ("x", "zl", "y", "zh", "c")
MESH = pl.DeviceIdType.MESH
ANY = pl.BlockSpec(memory_space=pl.ANY)
VM = pl.BlockSpec(memory_space=pltpu.VMEM)
SM = pl.BlockSpec(memory_space=pltpu.SMEM)
BF = jnp.bfloat16
F32 = jnp.float32
STEPS = (1, -1, 2)
DMA = pltpu.SemaphoreType.DMA
epsilon = 1e-05
LOG2E = 1.4426950408889634
SCALE = HEAD ** (-0.5)
NEG = -1e30
SDS = jax.ShapeDtypeStruct


def place():
    return {a: lax.axis_index(a) for a in AXES}


def moved(p, x=0, y=0, z=0, c=0):
    zz = lax.rem(p["zh"] * 2 + p["zl"] + z + 4, 4)
    return {
        "x": lax.rem(p["x"] + x + 4, 4),
        "zl": lax.rem(zz, 2),
        "y": lax.rem(p["y"] + y + 4, 4),
        "zh": zz // 2,
        "c": lax.rem(p["c"] + c, 2),
    }


def greet(peers):
    bar = pltpu.get_barrier_semaphore()
    for q in peers:
        pl.semaphore_signal(bar, inc=1, device_id=q, device_id_type=MESH)
    pl.semaphore_wait(bar, len(peers))


class Links:
    def __init__(self, p, sems, local=None):
        self.p, self.sems, self.n, self.sent = p, sems, 0, []
        self.local, self.m = local, 0

    def take(self):
        self.n += 1
        return self.sems.at[self.n - 1]

    def make(self, src, dst, to):
        return pltpu.make_async_remote_copy(
            src_ref=src,
            dst_ref=dst,
            send_sem=self.take(),
            recv_sem=self.take(),
            device_id=to,
            device_id_type=MESH,
        )

    def go(self, src, dst, to):
        cp = self.make(src, dst, to)
        cp.start()
        self.sent.append(cp)
        return cp

    def here(self, src, dst):
        self.m += 1
        cp = pltpu.make_async_copy(src, dst, self.local.at[self.m - 1])
        cp.start()
        return cp

    def finish(self):
        for cp in self.sent:
            cp.wait_send()
        self.sent = []


class TeamGather:
    def __init__(self, links, buf):
        p = links.p
        self.l, self.buf = links, buf
        self.up, self.down, self.twin = moved(p, y=1), moved(p, y=-1), moved(p, c=1)
        self.shared = []

    def block(self, d):
        return lax.rem(self.l.p["y"] + d + 4, 4) * 2 + self.l.p["c"]

    def go(self, kind, d, to):
        ref = self.buf.at[kind, self.block(d)]
        return self.l.go(ref, ref, to)

    def share(self, kind, d):
        self.shared.append(self.go(kind, d, self.twin))

    def begin(self):
        self.a0 = self.go(0, 0, self.up)
        self.b0 = self.go(1, 0, self.down)
        self.a1 = self.go(1, 0, self.up)
        self.b1 = self.go(0, 0, self.down)
        self.share(0, 0)
        self.share(1, 0)

    def relay(self):
        self.a0.wait_recv()
        self.a2 = self.go(0, -1, self.up)
        self.b0.wait_recv()
        self.b2 = self.go(1, 1, self.down)
        self.share(0, -1)
        self.share(1, 1)

    def near(self):
        self.a1.wait_recv()
        self.share(1, -1)
        self.b1.wait_recv()
        self.share(0, 1)

    def far(self):
        self.a2.wait_recv()
        self.share(0, 2)
        self.b2.wait_recv()
        self.share(1, 2)

    def end(self):
        for cp in self.shared:
            cp.wait_recv()

    def all(self):
        self.begin()
        self.relay()
        self.near()
        self.far()
        self.end()


def add_into(dst, terms, step=16):
    n = dst.shape[0]

    def body(i, _):
        rows = pl.ds(pl.multiple_of(i * step, step), step)
        total = terms[0][rows].astype(F32)
        for ref in terms[1:]:
            total = total + ref[rows].astype(F32)
        dst[rows] = total.astype(dst.dtype)
        return 0

    lax.fori_loop(0, n // step, body, 0)


class TeamReduce:
    order = (2, 1, -1, 0)

    @staticmethod
    def scratch(c):
        return [
            pltpu.VMEM((4, 2, 64, c), BF),
            pltpu.VMEM((4, 2, 64, c), BF),
            pltpu.VMEM((2, 64, c), BF),
            pltpu.VMEM((2, 2, 64, c), BF),
        ]

    def __init__(self, links, part, tw, keep, r2, r1):
        p = links.p
        self.l, self.part, self.tw, self.keep, self.r2, self.r1 = links, part, tw, keep, r2, r1
        self.up, self.down, self.twin = moved(p, y=1), moved(p, y=-1), moved(p, c=1)
        self.twins = []

    def row(self, k):
        return lax.rem(self.l.p["y"] + self.order[k] + 4, 4)

    def push(self, k):
        other = self.row(k) * 2 + 1 - self.l.p["c"]
        self.twins.append(
            [self.l.go(self.part.at[m, other], self.tw.at[k, m], self.twin) for m in range(2)]
        )

    def merge(self, k):
        mine = self.row(k) * 2 + self.l.p["c"]
        for m in range(2):
            self.twins[k][m].wait_recv()
            add_into(self.keep.at[k, m], [self.part.at[m, mine], self.tw.at[k, m]])
        if k == 0:
            self.f0 = self.l.go(self.keep.at[0, 0], self.r2.at[0], self.up)
            self.f1 = self.l.go(self.keep.at[0, 1], self.r2.at[1], self.down)
        if k == 1:
            self.u1 = self.l.go(self.keep.at[1, 1], self.r1.at[0, 1], self.up)
        if k == 2:
            self.d0 = self.l.go(self.keep.at[2, 0], self.r1.at[1, 0], self.down)

    def relay(self):
        self.f0.wait_recv()
        add_into(self.keep.at[1, 0], [self.keep.at[1, 0], self.r2.at[0]])
        self.u0 = self.l.go(self.keep.at[1, 0], self.r1.at[0, 0], self.up)
        self.f1.wait_recv()
        add_into(self.keep.at[2, 1], [self.keep.at[2, 1], self.r2.at[1]])
        self.d1 = self.l.go(self.keep.at[2, 1], self.r1.at[1, 1], self.down)

    def arrive(self):
        for cp in (self.u1, self.d0, self.u0, self.d1):
            cp.wait_recv()

    def terms(self, m):
        return [self.keep.at[3, m], self.r1.at[0, m], self.r1.at[1, m]]


class WeightGather:
    def __init__(self, links, buf):
        p = links.p
        self.l, self.buf = links, buf
        self.xp = [moved(p, x=d) for d in STEPS]
        self.zp = [moved(p, z=1), moved(p, z=-1)]
        self.x, self.z = {}, []

    def go(self, shard, h, r, to):
        ref = self.buf.at[shard, pl.ds(128 * h + 64 * r, 64)]
        return self.l.go(ref, ref, to)

    def shard(self, d):
        return lax.rem(self.l.p["x"] + d + 4, 4) * 2 + self.l.p["zl"]

    def send(self, r):
        self.x[r] = [[self.go(self.shard(0), h, r, to) for h in range(2)] for to in self.xp]

    def own(self, r):
        self.z += [self.go(self.shard(0), h, r, self.zp[h]) for h in range(2)]

    def pass_on(self, r):
        for k, d in enumerate(STEPS):
            for h in range(2):
                self.x[r][k][h].wait_recv()
                self.z.append(self.go(self.shard(-d), h, r, self.zp[h]))

    def end(self):
        for cp in self.z:
            cp.wait_recv()


class Broadcast:
    def __init__(self, links, src, buf):
        p = links.p
        self.l, self.src, self.buf = links, src, buf
        self.holder = p["zl"] == p["c"]
        self.source = jnp.logical_and(self.holder, p["x"] == p["y"])
        mine = pl.ds(pl.multiple_of(p["zh"] * 128, 128), 128)
        lower = pl.ds(pl.multiple_of(moved(p, z=-1)["zh"] * 128, 128), 128)
        self.mine = mine
        make = links.make
        self.x = [make(src.at[mine], buf.at[mine], moved(p, x=d)) for d in STEPS]
        self.z = [make(buf.at[mine], buf.at[mine], moved(p, z=d)) for d in (1, -1)]
        self.back = make(buf.at[lower], buf.at[lower], moved(p, z=1))

    def begin(self):
        @pl.when(self.source)
        def _():
            for cp in self.x:
                cp.start()
            self.l.here(self.src.at[self.mine], self.buf.at[self.mine]).wait()

    def across(self):
        p = self.l.p
        for k, d in enumerate(STEPS):

            @pl.when(jnp.logical_and(self.holder, lax.rem(p["x"] - d + 4, 4) == p["y"]))
            def _():
                self.x[k].wait_recv()

        @pl.when(self.holder)
        def _():
            for cp in self.z:
                cp.start()

    def back_on(self):
        @pl.when(jnp.logical_not(self.holder))
        def _():
            self.z[0].wait_recv()
            self.back.start()
            self.z[1].wait_recv()

    def end(self):
        @pl.when(self.holder)
        def _():
            self.back.wait_recv()
            for cp in self.z:
                cp.wait_send()

        @pl.when(jnp.logical_not(self.holder))
        def _():
            self.back.wait_send()

        @pl.when(self.source)
        def _():
            for cp in self.x:
                cp.wait_send()


def call(kernel, outs, ins, in_specs, out_specs, scratch, cid, sems, local=1, mb=60):
    return pl.pallas_call(
        kernel,
        out_shape=outs,
        in_specs=in_specs,
        out_specs=out_specs,
        scratch_shapes=list(scratch) + [DMA((sems,)), DMA((local,))],
        compiler_params=pltpu.CompilerParams(
            collective_id=cid, has_side_effects=True, vmem_limit_bytes=mb * 2**20
        ),
    )(*ins)


def dot(a, b):
    return jnp.dot(a, b, preferred_element_type=F32)


def dot_t(a, b):
    return lax.dot_general(a, b, (((1,), (1,)), ((), ())), preferred_element_type=F32)


def t_dot(a, b):
    return lax.dot_general(a, b, (((0,), (0,)), ((), ())), preferred_element_type=F32)


def qkv_kernel(tok, gain, shift, bias, wsrc, n1, wq, mixed, sems, local):
    p = place()
    t = p["y"] * 2 + p["c"]
    me = p["x"] * 2 + p["zl"]
    links = Links(p, sems, local)
    w = WeightGather(links, wq)
    own = [
        links.here(
            wsrc.at[:, pl.ds(pl.multiple_of(2048 * k + 256 * t, 256), 256)],
            wq.at[me, :, pl.ds(256 * k, 256)],
        )
        for k in range(3)
    ]
    g = TeamGather(links, n1)
    greet(tuple(w.xp + w.zp + [g.up, g.down, g.twin]))
    for cp in own:
        cp.wait()
    w.send(0)
    w.own(0)
    for m in range(2):
        v = tok[m].astype(F32)
        v = v - jnp.mean(v, axis=-1, keepdims=True)
        r = lax.rsqrt(jnp.mean(v * v, axis=-1, keepdims=True) + epsilon)
        n1[m, t] = (v * r * gain[...] + shift[...]).astype(BF)
    g.begin()
    w.send(1)
    w.own(1)
    g.relay()
    w.pass_on(0)
    g.near()
    g.far()
    w.pass_on(1)
    g.end()
    w.end()
    for i in range(8):
        m, b = i // 4, (i % 4) * 2
        rows = n1[m, b : b + 2].reshape(128, 2048)
        mixed[i * 128 : i * 128 + 128] = (
            dot(rows, wq[...].reshape(2048, 768)) + bias[...]
        ).astype(BF)
    links.finish()


def qkv_stage(tok, gain, shift, bias, wsrc, cid):
    return call(
        qkv_kernel,
        (SDS((2, 8, 64, 2048), BF), SDS((8, 256, 768), BF), SDS((1024, 768), BF)),
        (tok, gain, shift, bias, wsrc),
        [VM, VM, VM, VM, ANY],
        (VM, VM, VM),
        [],
        cid,
        128,
        3,
    )


def key_bias(dst, lens, slope, half, base=None):
    for b in range(8):
        v = lax.broadcasted_iota(jnp.int32, (128, 128), 0) + half * 128
        if b < 4:
            v = v + 256 * b
            live = v < lens[0, 0]
            v = v - lens[0, 0]
        else:
            live = v < lens[0, b - 3]
        dst[b * 128 : b * 128 + 128] = jnp.where(live, v.astype(F32) * slope, NEG)


def segments(b):
    if b < 4:
        out = [(0, 0, 128 * b, 0)] if b else []
        out += [(0, 128 * b, 128, 1)]
        out += [(1, 0, 128 * b, 0)] if b else []
        return out + [(1, 128 * b, 128, 2)]
    at = 512 + 128 * (b - 4)
    return [(0, 0, 512, 0), (1, 0, 512, 0), (0, at, 128, 1), (1, at, 128, 2)]


def score(seg, ks, biases, qb, tri, shut):
    far, at, n, kind = seg
    s = dot_t(ks[far][at : at + n], qb) * (SCALE * LOG2E) + biases[far][at : at + n]
    if kind == 1:
        s = jnp.where(tri, s, NEG)
    if kind == 2:
        s = s + shut
    return s


def triangle():
    shape = (128, 128)
    return lax.broadcasted_iota(jnp.int32, shape, 0) <= lax.broadcasted_iota(jnp.int32, shape, 1)


def attend_head(h, p, lens, slopes, mixed, far, heads, lse, bo, bf, vo, vf):
    cols = slice(128 * h, 128 * h + 128)
    slope = slopes[0, h]
    key_bias(bo, lens, slope, p["zh"])
    key_bias(bf, lens, slope, 1 - p["zh"])
    vo[...] = mixed[:, 512 + 128 * h : 640 + 128 * h].T
    vf[...] = far[:, 256 + 128 * h : 384 + 128 * h].T
    tri = triangle()
    shut = jnp.where(p["zh"] == 1, 0.0, NEG).astype(F32)
    ks = (mixed.at[:, pl.ds(256 + 128 * h, 128)], far.at[:, pl.ds(128 * h, 128)])
    for b in range(8):
        qb = mixed[b * 128 : b * 128 + 128, cols]
        segs = segments(b)
        s = [score(seg, ks, (bo, bf), qb, tri, shut) for seg in segs]
        top = functools.reduce(jnp.maximum, [jnp.max(v, axis=0, keepdims=True) for v in s])
        e = [jnp.exp2(v - top) for v in s]
        total = functools.reduce(jnp.add, [jnp.sum(v, axis=0, keepdims=True) for v in e])
        inv = 1.0 / total
        out = None
        for (side, at, n, _), v in zip(segs, e):
            vt = (vo, vf)[side][:, at : at + n]
            o = dot(vt, (v * inv).astype(BF))
            out = o if out is None else out + o
        heads[b * 128 : b * 128 + 128, cols] = out.T.astype(BF)
        lse[h * 8 + b : h * 8 + b + 1] = top + jnp.log2(total)


def attend_kernel(
    mixed, cot, lens, slopes, wo_src, wu_src, wd_src,
    heads, lse, far, dy, wo, wu, wd, bo, bf, vo, vf, sems, local,
):
    p = place()
    t = p["y"] * 2 + p["c"]
    me = p["x"] * 2 + p["zl"]
    links = Links(p, sems, local)
    wide = pl.ds(pl.multiple_of(1024 * t, 1024), 1024)
    own = [links.here(wu_src.at[:, wide], wu.at[me]), links.here(wd_src.at[:, wide], wd.at[me])]
    peer = moved(p, z=2)
    up, down = WeightGather(links, wu), WeightGather(links, wd)
    g = TeamGather(links, dy)
    greet(tuple(up.xp + up.zp + [g.up, g.down, g.twin, peer]))

    def swap(h):
        return [
            links.go(
                mixed.at[:, pl.ds(256 * k + 256 + 128 * h, 128)],
                far.at[:, pl.ds(256 * k + 128 * h, 128)],
                peer,
            )
            for k in range(2)
        ]

    first = swap(0)
    out = Broadcast(links, wo_src, wo)
    out.begin()
    for m in range(2):
        dy[m, t] = cot[m]
    g.begin()
    for cp in own:
        cp.wait()
    up.send(0)
    g.relay()
    for cp in first:
        cp.wait_recv()
    second = swap(1)
    out.across()
    up.send(1)
    g.near()
    g.far()
    attend_head(0, p, lens, slopes, mixed, far, heads, lse, bo, bf, vo, vf)
    out.back_on()
    for cp in second:
        cp.wait_recv()
    up.own(0)
    up.pass_on(0)
    down.send(0)
    attend_head(1, p, lens, slopes, mixed, far, heads, lse, bo, bf, vo, vf)
    up.own(1)
    up.pass_on(1)
    down.send(1)
    down.own(0)
    down.pass_on(0)
    down.own(1)
    down.pass_on(1)
    g.end()
    up.end()
    down.end()
    out.end()
    links.finish()


def attend_stage(mixed, cot, lens, slopes, wo, wu, wd, cid):
    v = pltpu.VMEM
    return call(
        attend_kernel,
        (
            SDS((1024, 256), BF),
            SDS((16, 128), F32),
            SDS((1024, 512), BF),
            SDS((2, 8, 64, 2048), BF),
            SDS((256, 2048), BF),
            SDS((8, 256, 1024), BF),
            SDS((8, 256, 1024), BF),
        ),
        (mixed, cot, lens, slopes, wo, wu, wd),
        [VM, VM, SM, SM, ANY, ANY, ANY],
        (VM, VM, VM, VM, VM, VM, VM),
        [v((1024, 128), F32), v((1024, 128), F32), v((128, 1024), BF), v((128, 1024), BF)],
        cid,
        200,
        3,
    )


def attend_back_head(h, p, lens, slopes, mixed, far, lse, dheads, dq, acc, bo, bf, ko, kf):
    cols = slice(128 * h, 128 * h + 128)
    slope = slopes[0, h]
    key_bias(bo, lens, slope, p["zh"])
    key_bias(bf, lens, slope, 1 - p["zh"])
    ko[...] = mixed[:, 256 + 128 * h : 384 + 128 * h].T
    kf[...] = far[:, 128 * h : 128 * h + 128].T
    acc[...] = jnp.zeros_like(acc)
    tri = triangle()
    shut = jnp.where(p["zh"] == 1, 0.0, NEG).astype(F32)
    ks = (mixed.at[:, pl.ds(256 + 128 * h, 128)], far.at[:, pl.ds(128 * h, 128)])
    vs = (mixed.at[:, pl.ds(512 + 128 * h, 128)], far.at[:, pl.ds(256 + 128 * h, 128)])
    for b in range(8):
        rows = slice(b * 128, b * 128 + 128)
        qb = mixed[rows, cols]
        do = dheads[rows, cols]
        log_total = lse[h * 8 + b : h * 8 + b + 1]
        segs = segments(b)
        probs = [jnp.exp2(score(seg, ks, (bo, bf), qb, tri, shut) - log_total) for seg in segs]
        dp = [dot_t(vs[side][at : at + n], do) for side, at, n, _ in segs]
        delta = functools.reduce(
            jnp.add, [jnp.sum(a * d, axis=0, keepdims=True) for a, d in zip(probs, dp)]
        )
        dqt = None
        for (side, at, n, _), a, d in zip(segs, probs, dp):
            ds = (a * (d - delta)).astype(BF)
            acc[side, 0, at : at + n] += dot(ds, qb)
            acc[side, 1, at : at + n] += dot(a.astype(BF), do)
            o = dot((ko, kf)[side][:, at : at + n], ds)
            dqt = o if dqt is None else dqt + o
        dq[rows, cols] = (dqt.T * SCALE).astype(BF)


def attend_back_kernel(
    mixed, far, lens, slopes, lse, dheads, heads,
    dqkv, hall, acc, keep, back, got, bo, bf, ko, kf, sems, local,
):
    p = place()
    t = p["y"] * 2 + p["c"]
    links = Links(p, sems, local)
    peer = moved(p, z=2)
    g = TeamGather(links, hall)
    greet((g.up, g.down, g.twin, peer))
    for m in range(2):
        hall[m, t] = heads[m * 512 : m * 512 + 512]
    g.begin()
    swaps = []
    for h in range(2):
        attend_back_head(h, p, lens, slopes, mixed, far, lse, dheads, dqkv, acc, bo, bf, ko, kf)
        cols = slice(128 * h, 128 * h + 128)
        back[h, 0] = (acc[1, 0] * SCALE).astype(BF)
        back[h, 1] = acc[1, 1].astype(BF)
        swaps.append(links.go(back.at[h], got.at[h], peer))
        if h == 0:
            g.relay()
            keep[...] = acc[0]
        else:
            g.near()
            g.far()
    swaps[0].wait_recv()
    dqkv[:, 256:384] = (keep[0] * SCALE + got[0, 0].astype(F32)).astype(BF)
    dqkv[:, 512:640] = (keep[1] + got[0, 1].astype(F32)).astype(BF)
    swaps[1].wait_recv()
    dqkv[:, 384:512] = (acc[0, 0] * SCALE + got[1, 0].astype(F32)).astype(BF)
    dqkv[:, 640:768] = (acc[0, 1] + got[1, 1].astype(F32)).astype(BF)
    g.end()
    links.finish()


def attend_back_stage(mixed, far, lens, slopes, lse, dheads, heads, cid):
    v = pltpu.VMEM
    return call(
        attend_back_kernel,
        (SDS((1024, 768), BF), SDS((2, 8, 512, 256), BF)),
        (mixed, far, lens, slopes, lse, dheads, heads),
        [VM, VM, SM, SM, VM, VM, VM],
        (VM, VM),
        [
            v((2, 2, 1024, 128), F32),
            v((2, 1024, 128), F32),
            v((2, 2, 1024, 128), BF),
            v((2, 2, 1024, 128), BF),
            v((1024, 128), F32),
            v((1024, 128), F32),
            v((128, 1024), BF),
            v((128, 1024), BF),
        ],
        cid,
        64,
    )


def gather_kernel(a, out, sems, local):
    p = place()
    t = p["y"] * 2 + p["c"]
    links = Links(p, sems, local)
    g = TeamGather(links, out)
    greet((g.up, g.down, g.twin))
    for m in range(2):
        out[m, t] = a[m]
    g.all()
    links.finish()


def gather_stage(a, cid):
    return call(
        gather_kernel, SDS((2, 8) + a.shape[1:], a.dtype), (a,), [VM], VM, [], cid, 32
    )


def reduce_kernel(part, out, tw, keep, r2, r1, sems, local):
    p = place()
    links = Links(p, sems, local)
    r = TeamReduce(links, part, tw, keep, r2, r1)
    greet((r.up, r.down, r.twin))
    for k in range(4):
        r.push(k)
    for k in range(4):
        r.merge(k)
    r.relay()
    r.arrive()
    for m in range(2):
        add_into(out.at[m], r.terms(m))
    links.finish()


def reduce_stage(part, cid):
    c = part.shape[-1]
    return call(
        reduce_kernel, SDS((2, 64, c), F32), (part,), [VM], VM, TeamReduce.scratch(c), cid, 40
    )


class GradReduce:
    @staticmethod
    def scratch(w):
        v, h = pltpu.VMEM, w // 2
        return [
            v((2, 256, h), BF),
            v((4, 128, h), BF),
            v((3, 2, 256, h), BF),
            v((3, 4, 128, h), BF),
            v((2, 256, h), BF),
            v((4, 128, h), BF),
            v((3, 128, h), BF),
            v((3, 128, h), BF),
        ]

    def __init__(self, links, g, out, ma, mb, rx1, rz1, s1, s2, rx2, rz2):
        self.l, self.g, self.out = links, g, out
        self.ma, self.mb, self.rx1, self.rz1 = ma, mb, rx1, rz1
        self.s1, self.s2, self.rx2, self.rz2 = s1, s2, rx2, rz2
        p = links.p
        w = g.shape[3] // 2
        self.ca, self.cb = pl.ds(0, w), pl.ds(w, w)
        self.xp = [moved(p, x=d) for d in STEPS]
        self.zp = [moved(p, z=d) for d in STEPS]

    @staticmethod
    def rows(q):
        return pl.ds(pl.multiple_of(q["zh"] * 128, 128), 128)

    def begin(self):
        g, p, go = self.g, self.l.p, self.l.go
        self.ax, self.az = [], []
        for k in (2, 0, 1):
            q = self.xp[k]
            self.ax.append(go(g.at[q["x"], :, :, self.ca], self.rx1.at[k], q))
            q = self.zp[k]
            self.az.append(go(g.at[:, q["zl"], self.rows(q), self.cb], self.rz1.at[k], q))
        self.la = self.l.here(g.at[p["x"], :, :, self.ca], self.ma)
        self.lb = self.l.here(g.at[:, p["zl"], self.rows(p), self.cb], self.mb)

    def middle_x(self):
        self.la.wait()
        for cp in self.ax:
            cp.wait_recv()
        for i in range(2):
            add_into(self.s1.at[i], [self.ma.at[i]] + [self.rx1.at[k, i] for k in range(3)])
        self.bz = [
            self.l.go(self.s1.at[q["zl"], self.rows(q)], self.rz2.at[k], q)
            for k, q in enumerate(self.zp)
        ]

    def middle_z(self):
        self.lb.wait()
        for cp in self.az:
            cp.wait_recv()
        for i in range(4):
            add_into(self.s2.at[i], [self.mb.at[i]] + [self.rz1.at[k, i] for k in range(3)])
        self.bx = [
            self.l.go(self.s2.at[q["x"]], self.rx2.at[k], q) for k, q in enumerate(self.xp)
        ]

    def end(self):
        p = self.l.p
        for cp in self.bz:
            cp.wait_recv()
        mine = self.s1.at[p["zl"], self.rows(p)]
        add_into(self.out.at[:, self.ca], [mine] + [self.rz2.at[k] for k in range(3)])
        for cp in self.bx:
            cp.wait_recv()
        add_into(self.out.at[:, self.cb], [self.s2.at[p["x"]]] + [self.rx2.at[k] for k in range(3)])


class Spread:
    def __init__(self, links, a, out):
        p = links.p
        self.l, self.a, self.out, self.zh = links, a, out, p["zh"]
        self.yp = [moved(p, y=d) for d in STEPS]
        self.far, self.twin = moved(p, z=2), moved(p, c=1)
        self.twins = []

    def at(self, far, d, half):
        zh = 1 - self.zh if far else self.zh
        b = lax.rem(self.l.p["y"] + d + 4, 4) * 2 + self.l.p["c"]
        return (zh, b, pl.ds(64 * half, 64))

    def share(self, src, at):
        self.twins.append(self.l.go(src, self.out.at[at], self.twin))

    def begin(self):
        go, out = self.l.go, self.out
        self.own = self.l.here(self.a, out.at[self.zh, self.at(0, 0, 0)[1]])
        lo, hi = self.a.at[pl.ds(0, 64)], self.a.at[pl.ds(64, 64)]
        self.first = [go(lo, out.at[self.at(0, 0, 0)], q) for q in self.yp]
        self.cross = go(hi, out.at[self.at(0, 0, 1)], self.far)
        self.firstz = [go(lo, out.at[self.at(0, 0, 0)], self.far)]
        self.second = [go(hi, out.at[self.at(0, 0, 1)], q) for q in self.yp]
        self.share(lo, self.at(0, 0, 0))
        self.share(hi, self.at(0, 0, 1))

    def middle(self):
        go, out = self.l.go, self.out
        for k, d in enumerate(STEPS):
            self.first[k].wait_recv()
            at = self.at(0, -d, 0)
            self.firstz.append(go(out.at[at], out.at[at], self.far))
            self.share(out.at[at], at)
        self.cross.wait_recv()
        at = self.at(1, 0, 1)
        self.third = [go(out.at[at], out.at[at], q) for q in self.yp]
        self.share(out.at[at], at)
        for k, d in enumerate(STEPS):
            self.second[k].wait_recv()
            at = self.at(0, -d, 1)
            self.share(out.at[at], at)

    def end(self):
        for k, d in enumerate((0,) + STEPS):
            self.firstz[k].wait_recv()
            at = self.at(1, -d, 0)
            self.share(self.out.at[at], at)
        for k, d in enumerate(STEPS):
            self.third[k].wait_recv()
            at = self.at(1, -d, 1)
            self.share(self.out.at[at], at)
        for cp in self.twins:
            cp.wait_recv()
        self.own.wait()


def grads_kernel(n, *refs):
    p = place()
    gs, outs, refs = refs[:n], refs[n : 2 * n], refs[2 * n :]
    sums, refs = refs[:n], refs[n:]
    sems, local = refs[-2:]
    links = Links(p, sems, local)
    rs = [
        GradReduce(links, gs[i], sums[i], *refs[8 * i : 8 * i + 8]) for i in range(n)
    ]
    ss = [Spread(links, sums[i], outs[i]) for i in range(n)]
    greet(tuple(rs[0].xp + rs[0].zp + ss[0].yp + [ss[0].twin]))
    for r in rs:
        r.begin()
    for r in rs:
        r.middle_x()
        r.middle_z()
    for r, s in zip(rs, ss):
        r.end()
        s.begin()
    for s in ss:
        s.middle()
    for s in ss:
        s.end()
    links.finish()


def grads_stage(gs, cid):
    gs = tuple(g.reshape(4, 2, 256, g.shape[-1]) for g in gs)
    ws = [g.shape[-1] for g in gs]
    n = len(gs)
    scratch = [pltpu.VMEM((128, w), BF) for w in ws]
    for w in ws:
        scratch += GradReduce.scratch(w)
    return call(
        functools.partial(grads_kernel, n),
        tuple(SDS((2, 8, 128, w), BF) for w in ws),
        gs,
        [ANY] * n,
        (ANY,) * n,
        scratch,
        cid,
        100 * n,
        3 * n,
    )


def widen_kernel(*refs):
    n = len(refs) // 2
    for a, o in zip(refs[:n], refs[n:]):
        o[...] = a[0, 0].astype(F32)


def widen(parts):
    ws = [a.shape[-1] for a in parts]
    return pl.pallas_call(
        widen_kernel,
        grid=(2, 8),
        out_shape=tuple(SDS((256, 8 * w), F32) for w in ws),
        in_specs=[pl.BlockSpec((1, 1, 128, w), lambda i, j: (i, j, 0, 0)) for w in ws],
        out_specs=tuple(pl.BlockSpec((128, w), lambda i, j: (i, j)) for w in ws),
    )(*parts)


def widen_qkv(part):
    return pl.pallas_call(
        widen_kernel,
        grid=(2, 3, 8),
        out_shape=SDS((256, 6144), F32),
        in_specs=[pl.BlockSpec((1, 1, 128, 256), lambda i, k, j: (i, j, 0, k))],
        out_specs=pl.BlockSpec((128, 256), lambda i, k, j: (i, k * 8 + j)),
    )(part)


def small_kernel(v, out, bx, bz, bc, by, sems, local):
    p = place()
    z = p["zh"] * 2 + p["zl"]
    links = Links(p, sems, local)
    xp = [moved(p, x=d) for d in STEPS]
    zp = [moved(p, z=d) for d in STEPS]
    yp = [moved(p, y=d) for d in STEPS]
    twin = moved(p, c=1)
    greet(tuple(xp + zp + yp + [twin]))

    def exchange(buf, at, peers):
        for cp in [links.go(buf.at[at], buf.at[at], q) for q in peers]:
            cp.wait_recv()

    bx[p["x"]] = v[...]
    exchange(bx, p["x"], xp)
    bz[z] = bx[0] + bx[1] + bx[2] + bx[3]
    exchange(bz, z, zp)
    bc[p["c"]] = bz[0] + bz[1] + bz[2] + bz[3]
    exchange(bc, p["c"], [twin])
    by[p["y"], 0:96] = bc[0, 0:96] + bc[1, 0:96]
    by[p["y"], 96:112] = bc[0, 96:112]
    by[p["y"], 112:128] = bc[1, 96:112]
    exchange(by, p["y"], yp)
    out[...] = by[...]
    links.finish()


def small_sums(v, cid):
    vm = pltpu.VMEM
    return call(
        small_kernel,
        SDS((4, 128, 128), F32),
        (v,),
        [VM],
        VM,
        [vm((4, 112, 128), F32), vm((4, 112, 128), F32), vm((2, 112, 128), F32), vm((4, 128, 128), F32)],
        cid,
        24,
    )


def norm_rows(values, gain, shift):
    average = jnp.mean(values, axis=-1, keepdims=True)
    centred = values - average
    variance = jnp.mean(centred * centred, axis=-1, keepdims=True)
    return centred * lax.rsqrt(variance + epsilon) * gain + shift


def gelu_tanh(values):
    return jax.nn.gelu(values, approximate=True)


def body(
    tokens,
    cotangent,
    lengths,
    qkv_weight,
    out_weight,
    up_weight,
    down_weight,
    bias_query,
    bias_value,
    out_bias,
    up_bias,
    down_bias,
    norm_gain_one,
    norm_shift_one,
    norm_gain_two,
    norm_shift_two,
):
    p = place()
    t = p["y"] * 2 + p["c"]
    out_b = out_bias.astype(F32)
    down_b = down_bias.astype(F32)
    gain_one = norm_gain_one.astype(F32).reshape(1, 2048)
    shift_one = norm_shift_one.astype(F32).reshape(1, 2048)
    gain_two = norm_gain_two.astype(F32)
    shift_two = norm_shift_two.astype(F32)

    def cut(v, n):
        return lax.dynamic_slice_in_dim(v, t * n, n, v.ndim - 1)

    def blocks(v):
        return v.reshape(2, 8, 64, 2048)

    toks = tokens.reshape(2, 64, 2048)
    cots = cotangent.reshape(2, 64, 2048)
    qb = cut(bias_query, 256).astype(F32)
    vb = cut(bias_value, 256).astype(F32)
    bias_cat = jnp.concatenate([qb, jnp.zeros_like(qb), vb]).reshape(1, 768)
    slopes = jnp.exp2(-8.0 * (t * 2 + jnp.arange(2, dtype=jnp.int32) + 1).astype(F32) / H)
    slopes = (slopes * LOG2E).reshape(1, 2)
    n1, w_qkv, mixed = qkv_stage(toks, gain_one, shift_one, bias_cat, qkv_weight, 0)
    heads, lse, far, dy, w_out, w_up, w_down = attend_stage(
        mixed, cots, lengths, slopes, out_weight, up_weight, down_weight, 1
    )
    n1 = n1.reshape(1024, 2048)
    dy = dy.reshape(1024, 2048)
    w_qkv = w_qkv.reshape(2048, 768)
    w_up = w_up.reshape(2048, 1024)
    w_down = w_down.reshape(2048, 1024)
    tok = toks.astype(F32)
    normed, norm_one_back = jax.vjp(norm_rows, tok, gain_one, shift_one)

    attended = reduce_stage(blocks(dot(heads, w_out).astype(BF)), 2)
    middle = tok + attended + out_b
    normed_two, norm_two_back = jax.vjp(norm_rows, middle, gain_two, shift_two)
    n2 = gather_stage(normed_two.astype(BF), 3).reshape(1024, 2048)
    hidden = dot(n2, w_up) + cut(up_bias, 1024).astype(F32)
    activated, gelu_back = jax.vjp(gelu_tanh, hidden)
    act = activated.astype(BF)
    branch = reduce_stage(blocks(dot_t(act, w_down).astype(BF)), 4)
    output = (middle + branch + down_b).astype(BF).reshape(128, 2048)
    (pre_grad,) = gelu_back(dot(dy, w_down))
    dpre = pre_grad.astype(BF)
    dn2 = reduce_stage(blocks(dot_t(dpre, w_up).astype(BF)), 5)
    mid_norm, gain_two_grad, shift_two_grad = norm_two_back(dn2)
    dmiddle = cots.astype(F32) + mid_norm
    dattn_own = dmiddle.astype(BF)
    dattn = gather_stage(dattn_own, 6).reshape(1024, 2048)
    dheads = dot_t(dattn, w_out).astype(BF)
    dqkv, hall = attend_back_stage(mixed, far, lengths, slopes, lse, dheads, heads, 7)
    dn1 = reduce_stage(blocks(dot_t(dqkv, w_qkv).astype(BF)), 8)
    token_norm, gain_one_grad, shift_one_grad = norm_one_back(dn1)
    input_grad = (dmiddle + token_norm).astype(BF).reshape(128, 2048)
    dcut = cut(dattn, 256).reshape(2, 512, 256)
    g_out = jnp.einsum("mtrf,mro->tfo", hall, dcut, preferred_element_type=F32).astype(BF)
    g_up, g_down = grads_stage((t_dot(n2, dpre).astype(BF), t_dot(dy, act).astype(BF)), 9)
    g_qkv, g_out = grads_stage((t_dot(n1, dqkv).astype(BF), g_out.reshape(2048, 256)), 10)
    up_grad, down_grad = widen((g_up, g_down))
    (out_grad,) = widen((g_out,))
    qkv_grad = widen_qkv(g_qkv)

    def total(v):
        return jnp.sum(v.astype(F32).reshape(-1, v.shape[-1]), axis=0)

    rows = jnp.concatenate(
        [
            total(dattn_own),
            total(cotangent),
            gain_one_grad.reshape(2048),
            shift_one_grad.reshape(2048),
            gain_two_grad,
            shift_two_grad,
        ]
    ).reshape(96, 128)
    dqkv_sum = total(dqkv)
    cols = jnp.concatenate(
        [total(dpre), dqkv_sum[:256], dqkv_sum[512:], jnp.zeros((512,), F32)]
    ).reshape(16, 128)
    sums = small_sums(jnp.concatenate([rows, cols]), 11)
    rows = (sums[0, :96] + sums[1, :96] + sums[2, :96] + sums[3, :96]).reshape(6, 2048)
    cols = sums[:, 96:].reshape(8, 2048)
    return (
        output,
        input_grad,
        qkv_grad,
        out_grad,
        up_grad,
        down_grad,
        cols[:, 1024:1280].reshape(2048),
        cols[:, 1280:1536].reshape(2048),
        rows[0],
        cols[:, :1024].reshape(8192),
        rows[1],
        rows[2],
        rows[3],
        rows[4],
        rows[5],
    )


def solution(mesh):
    fine = Mesh(mesh.devices.reshape(4, 2, 4, 2, 2), AXES)
    tok = P(AXES, None)
    row = P(("x", "zl"), None)
    in_specs = (tok, tok, row, row, row, row, row) + (P(),) * 9
    out_specs = (tok, tok, row, row, row, row) + (P(),) * 9
    return jax.shard_map(body, mesh=fine, in_specs=in_specs, out_specs=out_specs, check_vma=False)
```

time: 4570 us -> 676 us (0.15)
  waiting for transfers between devices: 4130 us -> 0 us
  Pallas kernels: 0 us -> 557 us
  matrix products: 208 us -> 77.9 us
  other arithmetic: 89.7 us -> 20.6 us
  local copies, waits for them, and re-layouts: 58.5 us -> 6.83 us
    all_gather x4 -> x0, waiting for transfers between devices: 1840 us -> none  [the longest x1 642 us: body(): lax.all_gather(down_weight, 'dp', axis=0, tiled=True)]
    reduce_scatter x2 -> x0, waiting for transfers between devices: 1840 us -> none  [the longest x1 1270 us: body(): lax.psum_scatter(jnp.concatenate([contract_rows(normed_two_low, pre_low),...]
    pallas_call x0 -> x15, Pallas kernels: none -> 557 us  [the longest x12 509 us: call(): pl.pallas_call(kernel, out_shape=outs, in_specs=in_specs, out_specs=out_s...]
    psum x2 -> x0, waiting for transfers between devices: 381 us -> none  [the longest x1 248 us: body(): lax.psum(attn_part, 'seq').astype(jnp.float32)]
    dot_general x40 -> x11, matrix products: 208 us -> 77.9 us  [the longest x4 28.9 us: dot_t(): lax.dot_general(a, b, (((1,), (1,)), ((), ())), preferred_element_type=F32)]
    all_to_all x4 -> x0, waiting for transfers between devices: 68.8 us -> none  [the longest x1 21.9 us: body(): lax.all_to_all(mixed.reshape(per_device, 3, H, HEAD), 'seq', split_axis=2...]
    concatenate x3 -> x2, other arithmetic: 66.8 us -> 0.02 us  [the longest x1 0.01 us: body(): bias_cat = jnp.concatenate([qb, jnp.zeros_like(qb), vb]).reshape(1, 768)]
  transfers between devices with their start and end apart: 12 -> 0, of which waited for: 12 -> 0; matrix products, arithmetic and copies ran while one was open for 4% -> 0% of each run, Pallas kernels for 0% -> 0%
where the time goes in v2:
time: 676 us; the launch traced here: 664 us
  Pallas kernels  557 us (82%)
  matrix products  77.9 us (12%)
  other arithmetic  20.6 us (3%)
  local copies, waits for them, and re-layouts  6.83 us (1%)
    pallas_call x12, Pallas kernels, call(): pl.pallas_call(kernel, out_shape=outs, in_specs=in_specs, out_specs=out_s...  509 us
    dot_general x4, matrix products, dot_t(): lax.dot_general(a, b, (((1,), (1,)), ((), ())), preferred_element_type=F32)  28.9 us
    dot_general x3, matrix products, dot(): return jnp.dot(a, b, preferred_element_type=F32)  26.6 us
    pallas_call x1, Pallas kernels, widen_qkv(): pl.pallas_call(widen_kernel, grid=(2, 3, 8), out_shape=SDS((256, 6144), F...  25.3 us
    pallas_call x2, Pallas kernels, widen(): pl.pallas_call(widen_kernel, grid=(2, 8), out_shape=tuple((SDS((256, 8 *...  22.2 us
    dot_general x3, matrix products, t_dot(): lax.dot_general(a, b, (((0,), (0,)), ((), ())), preferred_element_type=F32)  20.2 us

profile of v2, /device:TPU:1, one launch (start us, length us, event | category | flops | bytes accessed | tf_op | source)
XLA Modules:
  0.0 663.6 jit_solution(9902849677815667989)
XLA Ops:
  0.6 0.7 convert_element_type.110
  1.3 0.7 convert_element_type.109
  2.0 1.3 convert_element_type.103
  3.3 1.3 reshape.286
  4.6 0.8 dynamic-slice_convert_fusion.1
  6.0 42.4 %shard_map.271 = (bf16[2,8,64,2048]{3,2,1,0:T(8,128)(2,1)}, bf16[8,256,768]{2,1,0:T(8,128)(2,1)}, bf16[1024,768]{1,0:T(8,128)(2,1)}) custom-call(bf16[2,64,2048]{2,1,0:T(8,128)(2,1)} %bitcast.94, f32[1,2048]{1,0:T(1,128)} %bitcast.113, f32[1,2048]{1,0:T(1,128)} %bitcast.114, f32[1,768]{1,0:T(1,128)} %reshape.262.bias, bf16[256,6144]{1,0:T(8,128)(2,1)} %wsrc.1), custom_call_target="tpu_custom_call" | custom-call | tf_op jit(solution)/shard_map/pallas_call | solution.py:305
  48.9 90.2 %shard_map.272 = (bf16[1024,256]{1,0:T(8,128)(2,1)}, f32[16,128]{1,0:T(8,128)}, bf16[1024,512]{1,0:T(8,128)(2,1)}, bf16[2,8,64,2048]{3,2,1,0:T(8,128)(2,1)}, bf1...) custom-call(bf16[1024,768]{1,0:T(8,128)(2,1)} %get-tuple-element.33.mixed, ...), custom_call_target="tpu_custom_call" | custom-call | tf_op jit(solution)/shard_map/pallas_call | solution.py:305
  139.2 4.9 convolution_convert_fusion
  144.1 28.2 %shard_map.273 = f32[2,64,2048]{2,1,0:T(8,128)} custom-call(bf16[2,8,64,2048]{3,2,1,0:T(8,128)(2,1)} %bitcast.97), custom_call_target="tpu_custom_call" | custom-call | tf_op jit(solution)/shard_map/pallas_call | solution.py:305
  172.4 1.4 fusion.13
  174.2 1.1 add_convert_fusion.2.a
  175.3 25.9 %shard_map.274 = bf16[2,8,64,2048]{3,2,1,0:T(8,128)(2,1)} custom-call(bf16[2,64,2048]{2,1,0:T(8,128)(2,1)} %add_convert_fusion.2.a), custom_call_target="tpu_custom_call" | custom-call | tf_op jit(solution)/shard_map/pallas_call | solution.py:305
  201.3 10.0 %fusion.24 = f32[1024,1024]{1,0:T(8,128)} fusion(bf16[1024,2048]{1,0:T(8,128)(2,1)} %bitcast.104, bf16[2048,1024]{1,0:T(8,128)(2,1)} %bitcast.123), kind=kOutput, calls=%fused_computation.84 | convolution fusion | flops 4294967296 | bytes 12582912 | tf_op jit(solution)/shard_map/dot_general | solution.py:318
  211.2 0.7 dynamic-slice_convert_fusion
  211.9 11.7 %convert_reduce_fusion = (f32[1024]{0:T(1024)S(1)}, bf16[1024,1024]{1,0:T(8,128)(2,1)S(1)}) fusion(f32[1024,1024]{1,0:T(8,128)} %fusion.24, f32[1024]{0:T(1024)S(1)} %dynamic-slice_convert_fusion, bf16[1024,2048]{1,0:T(8,128)(2,1)} %bitcast.118, bf16[2048,1024]{1,0:T(8,128)(2,1)} %bitcast.121), kind=kOutput, calls=%fused_computation.9 | convolution fusion | flops 4319083520 | bytes 14688256 | tf_op jit(solution)/shard_map/dot_general | solution.py:318
  223.6 6.1 convolution_convert_fusion.4
  229.8 37.6 %shard_map.276 = f32[2,64,2048]{2,1,0:T(8,128)} custom-call(bf16[2,8,64,2048]{3,2,1,0:T(8,128)(2,1)} %bitcast.101), custom_call_target="tpu_custom_call" | custom-call | tf_op jit(solution)/shard_map/pallas_call | solution.py:305
  267.4 1.6 multiply_reduce_fusion
  269.1 10.5 %convolution_convert_fusion.5 = bf16[1024,2048]{1,0:T(8,128)(2,1)} fusion(bf16[2048,1024]{1,0:T(8,128)(2,1)} %bitcast.122, f32[1024,1024]{1,0:T(8,128)} %fusion.24, f32[1024]{0:T(1024)S(1)} %dynamic-slice_convert_fusion), kind=kOutput, calls=%fused_computation.16 | convolution fusion | flops 4307550208 | bytes 12587008 | tf_op jit(solution)/shard_map/dot_general | solution.py:322
  279.5 26.6 %shard_map.275 = f32[2,64,2048]{2,1,0:T(8,128)} custom-call(bf16[2,8,64,2048]{3,2,1,0:T(8,128)(2,1)} %bitcast.102), custom_call_target="tpu_custom_call" | custom-call | tf_op jit(solution)/shard_map/pallas_call | solution.py:305
  306.1 2.4 fusion.22
  308.5 1.0 copy-done.4
  309.5 1.0 convert_reduce_fusion.4
  310.5 25.9 %shard_map.277 = bf16[2,8,64,2048]{3,2,1,0:T(8,128)(2,1)} custom-call(bf16[2,64,2048]{2,1,0:T(8,128)(2,1)} %get-tuple-element.61.a), custom_call_target="tpu_custom_call" | custom-call | tf_op jit(solution)/shard_map/pallas_call | solution.py:305
  336.4 4.3 convolution_convert_fusion.7.dheads
  340.7 36.3 %shard_map.278 = (bf16[1024,768]{1,0:T(8,128)(2,1)}, bf16[2,8,512,256]{3,2,1,0:T(8,128)(2,1)}) custom-call(bf16[1024,768]{1,0:T(8,128)(2,1)} %get-tuple-element.33.mixed, bf16[1024,512]{1,0:T(8,128)(2,1)} %get-tuple-element.39.far, s32[1,5]{1,0:T(1,128)} %lens.3, f32[1,2]{1,0:T(1,128)} %exponential_multiply_fusion.slopes, f32[16,128]{1,0:T(8,128)} %get-tuple-element.40.lse, ...), custom_call_target="tpu_custom_call" | custom-call | tf_op jit(solution)/shard_map/pallas_call | solution.py:305
  377.0 8.0 %convolution_convert_fusion.1 = bf16[1024,2048]{1,0:T(8,128)(2,1)} fusion(bf16[1024,768]{1,0:T(8,128)(2,1)} %get-tuple-element.41, bf16[2048,768]{1,0:T(8,128)(2,1)} %bitcast.125), kind=kOutput, calls=%fused_computation.12 | convolution fusion | flops 3223322624 | bytes 8912896 | tf_op jit(solution)/shard_map/dot_general | solution.py:322
  385.1 26.5 %shard_map.279 = f32[2,64,2048]{2,1,0:T(8,128)} custom-call(bf16[2,8,64,2048]{3,2,1,0:T(8,128)(2,1)} %bitcast.103), custom_call_target="tpu_custom_call" | custom-call | tf_op jit(solution)/shard_map/pallas_call | solution.py:305
  411.8 1.6 fusion.19
  413.8 2.0 fusion.12
  415.8 1.3 add_convert_fusion
  417.1 4.9 convolution_convert_fusion.6
  422.0 1.1 constant_dynamic-slice_fusion
  423.1 2.3 bitcast_convert_fusion
  425.4 55.3 %shard_map.280 = (bf16[2,8,128,768]{3,2,1,0:T(8,128)(2,1)}, bf16[2,8,128,256]{3,2,1,0:T(8,128)(2,1)}) custom-call(bf16[4,2,256,768]{3,2,1,0:T(8,128)(2,1)} %bitcast.108, bf16[4,2,256,256]{3,2,1,0:T(8,128)(2,1)} %bitcast.109), custom_call_target="tpu_custom_call" | custom-call | tf_op jit(solution)/shard_map/pallas_call | solution.py:305
  480.7 25.3 %shard_map.281 = f32[256,6144]{1,0:T(8,128)} custom-call(bf16[2,8,128,768]{3,2,1,0:T(8,128)(2,1)} %get-tuple-element.45.refs_0_), custom_call_target="tpu_custom_call" | custom-call | tf_op jit(solution)/shard_map/pallas_call | solution.py:863
  506.0 9.0 %shard_map.282 = f32[256,2048]{1,0:T(8,128)} custom-call(bf16[2,8,128,256]{3,2,1,0:T(8,128)(2,1)} %get-tuple-element.46.refs_0_), custom_call_target="tpu_custom_call" | custom-call | tf_op jit(solution)/shard_map/pallas_call | solution.py:853
  515.1 8.5 %convolution_convert_fusion.3 = bf16[2048,1024]{1,0:T(8,128)(2,1)} fusion(bf16[1024,2048]{1,0:T(8,128)(2,1)} %bitcast.105, bf16[1024,1024]{1,0:T(8,128)(2,1)S(1)} %copy-done.20), kind=kOutput, calls=%fused_computation.14 | convolution fusion | flops 4297064448 | bytes 10485760 | tf_op jit(solution)/shard_map/dot_general | solution.py:326
  523.5 6.8 %convolution_convert_fusion.2 = bf16[2048,1024]{1,0:T(8,128)(2,1)} fusion(bf16[1024,2048]{1,0:T(8,128)(2,1)S(1)} %bitcast.119, f32[1024,1024]{1,0:T(8,128)S(1)} %copy-done.18, f32[1024]{0:T(1024)S(1)} %dynamic-slice_convert_fusion), kind=kOutput, calls=%fused_computation.13 | convolution fusion | flops 4307550208 | bytes 12587008 | tf_op jit(solution)/shard_map/dot_general | solution.py:326
  530.3 94.9 %shard_map.283 = (bf16[2,8,128,1024]{3,2,1,0:T(8,128)(2,1)}, bf16[2,8,128,1024]{3,2,1,0:T(8,128)(2,1)}) custom-call(bf16[4,2,256,1024]{3,2,1,0:T(8,128)(2,1)} %bitcast.106, bf16[4,2,256,1024]{3,2,1,0:T(8,128)(2,1)} %bitcast.107), custom_call_target="tpu_custom_call" | custom-call | tf_op jit(solution)/shard_map/pallas_call | solution.py:305
  625.2 13.2 %shard_map.284 = (f32[256,8192]{1,0:T(8,128)}, f32[256,8192]{1,0:T(8,128)}) custom-call(bf16[2,8,128,1024]{3,2,1,0:T(8,128)(2,1)} %get-tuple-element.47.refs_0_, bf16[2,8,128,1024]{3,2,1,0:T(8,128)(2,1)} %get-tuple-element.48.refs_1_), custom_call_target="tpu_custom_call" | custom-call | tf_op jit(solution)/shard_map/pallas_call | solution.py:853
  638.9 0.6 copy-done.11
  639.5 19.5 %shard_map.285 = f32[4,128,128]{2,1,0:T(8,128)} custom-call(f32[112,128]{1,0:T(8,128)} %copy-done.11), custom_call_target="tpu_custom_call" | custom-call | tf_op jit(solution)/shard_map/pallas_call | solution.py:305
  658.9 0.9 slice.62
  659.8 0.6 copy.34
  661.0 0.9 slice_add_fusion
  661.9 0.6 slice_bitcast_fusion.1
  662.5 0.6 copy.38
  (75 shorter events, 3.3 us)
Async XLA Ops:
  144.1 28.3 %copy-start.12 = (bf16[2048]{0:T(1024)(128)(2,1)S(1)}, bf16[2048]{0:T(1024)(128)(2,1)}, u32[]{:S(2)}) copy-start(bf16[2048]{0:T(1024)(128)(2,1)} %param.25) | copy-start | bytes 12292
  144.1 28.3 %copy-start = (bf16[128,2048]{1,0:T(8,128)(2,1)S(1)}, bf16[128,2048]{1,0:T(8,128)(2,1)}, u32[]{:S(2)}) copy-start(bf16[128,2048]{1,0:T(8,128)(2,1)} %param.16) | copy-start | bytes 1572868
  172.3 1.9 copy-start.2
  211.9 11.7 %copy-start.17 = (bf16[8,256,1024]{2,1,0:T(8,128)(2,1)S(1)}, bf16[8,256,1024]{2,1,0:T(8,128)(2,1)}, u32[]{:S(2)}) copy-start(bf16[8,256,1024]{2,1,0:T(8,128)(2,1)} %get-tuple-element.36) | copy-start | bytes 12582916
  223.6 6.1 copy-start.19
  229.7 39.3 %copy-start.13 = (bf16[2048]{0:T(1024)(128)(2,1)S(1)}, bf16[2048]{0:T(1024)(128)(2,1)}, u32[]{:S(2)}) copy-start(bf16[2048]{0:T(1024)(128)(2,1)} %param.27) | copy-start | bytes 12292
  279.5 26.6 %copy-start.3 = (f32[2,64,2048]{2,1,0:T(8,128)S(1)}, f32[2,64,2048]{2,1,0:T(8,128)}, u32[]{:S(2)}) copy-start(f32[2,64,2048]{2,1,0:T(8,128)} %shard_map.276) | copy-start | bytes 3145732
  279.5 30.0 %copy-start.6 = (bf16[128,2048]{1,0:T(8,128)(2,1)S(1)}, bf16[128,2048]{1,0:T(8,128)(2,1)}, u32[]{:S(2)}) copy-start(bf16[128,2048]{1,0:T(8,128)(2,1)} %param.17) | copy-start | bytes 1572868
  308.5 1.0 copy-start.4
  308.5 27.9 %copy-start.9 = (bf16[256,2048]{1,0:T(8,128)(2,1)S(1)}, bf16[256,2048]{1,0:T(8,128)(2,1)}, u32[]{:S(2)}) copy-start(bf16[256,2048]{1,0:T(8,128)(2,1)} %get-tuple-element.35) | copy-start | bytes 3145732
  385.1 26.8 %copy-start.10 = (f32[2048]{0:T(1024)S(1)}, f32[2048]{0:T(1024)}, u32[]{:S(2)}) copy-start(f32[2048]{0:T(1024)} %convert_element_type.103) | copy-start | bytes 24580
  385.1 30.7 %copy-start.5 = (f32[2,64,2048]{2,1,0:T(8,128)S(1)}, f32[2,64,2048]{2,1,0:T(8,128)}, u32[]{:S(2)}) copy-start(f32[2,64,2048]{2,1,0:T(8,128)} %copy-done.4) | copy-start | bytes 3145732
  411.6 4.2 copy-start.1
  413.8 3.3 copy-start.7
  413.8 3.3 copy-start.15
  417.1 6.0 copy-start.16
  480.7 34.3 %copy-start.20 = (bf16[1024,1024]{1,0:T(8,128)(2,1)S(1)}, bf16[1024,1024]{1,0:T(8,128)(2,1)}, u32[]{:S(2)}) copy-start(bf16[1024,1024]{1,0:T(8,128)(2,1)} %copy-done.19) | copy-start | bytes 6291460
  515.1 8.5 %copy-start.14 = (bf16[2,8,64,2048]{3,2,1,0:T(8,128)(2,1)S(1)}, bf16[2,8,64,2048]{3,2,1,0:T(8,128)(2,1)}, u32[]{:S(2)}) copy-start(bf16[2,8,64,2048]{3,2,1,0:T(8,128)(2,1)} %get-tuple-element.38) | copy-start | bytes 12582916
  515.1 8.5 %copy-start.18 = (f32[1024,1024]{1,0:T(8,128)S(1)}, f32[1024,1024]{1,0:T(8,128)}, u32[]{:S(2)}) copy-start(f32[1024,1024]{1,0:T(8,128)} %fusion.24) | copy-start | bytes 12582916
  625.2 13.3 %copy-start.8 = (bf16[1024,768]{1,0:T(8,128)(2,1)S(1)}, bf16[1024,768]{1,0:T(8,128)(2,1)}, u32[]{:S(2)}) copy-start(bf16[1024,768]{1,0:T(8,128)(2,1)} %get-tuple-element.41) | copy-start | bytes 4718596
  638.9 0.6 copy-start.11
